TPU v7x, 32 devices: a whole 2x2x4 slice. The times are simulated.
32 devices in a mesh: occ: 4 (over x, core), vir: 8 (over z, y).
Axes of the slice: x: 2, y: 2, z: 4, core: 2. Of those that a mesh axis runs over, the one named last changes fastest.
Arguments:
- integrals: bfloat16 [16, 3072, 4, 3072], P('occ', 'vir'), may hold values from -0.15625 to 0.15625
- amplitudes: bfloat16 [4, 3072, 2048], P(None, 'vir', 'occ'), may hold values from -6 to 6
- irrep_labels: int32 [3072], replicated, may hold values from 0 to 7, as said below
Outputs:
- ladder: bfloat16 [16, 3072, 2048], P(None, 'vir', 'occ')
Inputs may be any that keep to these rules, and one draw needn't show every extreme that they name: `irrep_labels`: every label from 0 to 7 occurs; no label is held by more than 768 orbitals, and one label by exactly that many.
All inputs are finite; a program needn't handle non-finite values.
Results may differ from a plain program's by a relative error of at most 0.001.
Values may be sent and summed in bfloat16 or wider, within the bound.
No kernel may reach another device: no remote copies, remote signals or barrier semaphores. Data moves between devices by JAX's collectives and lax.ppermute only.
A program may use at most 640 MiB of HBM per device.

v0:
```python
import functools

import jax
import jax.numpy as jnp
from jax import lax
from jax.experimental import pallas as pl
from jax.experimental.pallas import tpu as pltpu
from jax.sharding import PartitionSpec as P

LABELS = 8
TILE = 128
RUN = 4
TILES = 4
GROUP = RUN * TILES
PIECE = 16
STRIDE = 1024
VMEM = 56 * 2**20
COST = pl.CostEstimate(flops=10**6, bytes_accessed=10**6, transcendentals=0)
CHUNKS = ((56, 6), (128, 12), (128, 12), (152, 18))


def before(values):
    count = values.shape[0]
    earlier = jnp.arange(count)[:, None] > jnp.arange(count)[None, :]
    earlier = earlier.reshape(earlier.shape + (1,) * (values.ndim - 1))
    return jnp.sum(jnp.where(earlier, values[None], 0), axis=1)


def slots_of(shard):
    return -(-(shard + LABELS * 2 * (PIECE - 1)) // TILE) * TILE


def make_plan(labels, rows, vir, shard):
    total = labels.shape[0]
    blocks = total // TILE
    names = jnp.arange(LABELS)
    member = labels.reshape(1, blocks, TILE) == names[:, None, None]
    lower = jnp.arange(TILE)[:, None] < jnp.arange(TILE)[None, :]
    within = jnp.dot(
        member.astype(jnp.bfloat16).reshape(LABELS * blocks, TILE),
        lower.astype(jnp.bfloat16),
        preferred_element_type=jnp.float32,
    )
    within = within.reshape(LABELS, blocks, TILE).astype(jnp.int32)
    held = jnp.sum(member.astype(jnp.int32), axis=2)
    held_before = before(held.T).T
    rank = jnp.sum(jnp.where(member, within + held_before[:, :, None], 0), axis=0).reshape(total)
    sizes = jnp.sum(held, axis=1)
    depth = (sizes + TILE - 1) // TILE

    shards = total // shard
    part = jnp.sum(held.reshape(LABELS, shards, shard // TILE), axis=2)
    part_before = before(part.T).T
    pieces = jnp.where(part > 0, (part_before % PIECE + part + PIECE - 1) // PIECE, 0)
    piece_from = before(pieces)
    piece_to = part_before // PIECE
    move = PIECE * (piece_from - piece_to)
    slot = rank.reshape(shards, shard) + jnp.sum(
        jnp.where(member.reshape(LABELS, shards, shard), move[:, :, None], 0), axis=0
    )

    slices = total // rows
    mine = labels.reshape(1, slices, rows) == names[:, None, None]
    count = jnp.sum(mine.astype(jnp.int32), axis=2)
    row_tiles = (count + RUN - 1) // RUN
    groups = (count + GROUP - 1) // GROUP
    group_from = before(groups)
    unit_from = before(row_tiles * depth[:, None])
    most = rows // GROUP + LABELS + 1
    at = jnp.arange(most)[None, :, None]
    inside = (at >= group_from[:, None]) & (at < (group_from + groups)[:, None])

    def pick(values):
        return jnp.sum(jnp.where(inside, values, 0), axis=0)

    order = jnp.where(inside, at - group_from[:, None], 0)
    group_tiles = pick(jnp.clip(row_tiles[:, None] - TILES * order, 0, TILES))
    group_depth = pick(depth[:, None, None])
    group_unit = pick(unit_from[:, None] + order * TILES * depth[:, None, None])
    group_label = pick(names[:, None, None])
    label_end = pick((group_from + groups)[:, None])
    label_turn = pick(jnp.cumsum((groups > 0).astype(jnp.int32), axis=0)[:, None])
    group_end = group_unit + group_tiles * group_depth
    live = jnp.sum(groups, axis=0)
    valid = jnp.arange(most)[:, None] < live[None]
    starts, bases = [jnp.zeros_like(live)], [jnp.zeros_like(live)]
    for size, steps in CHUNKS:
        fits = valid & (group_end <= (bases[-1] + size)[None])
        fits = fits & (jnp.arange(most)[:, None] < (starts[-1] + steps)[None])
        starts.append(jnp.sum(fits.astype(jnp.int32), axis=0))
        bases.append(jnp.max(jnp.where(fits, group_end, 0), axis=0))
    overflow = jnp.max(live - starts[-1]) > 0
    starts.append(live)
    starts, bases = jnp.stack(starts), jnp.stack(bases)
    chunk = jnp.sum((jnp.arange(most)[:, None, None] >= starts[None, 1:-1]).astype(jnp.int32), axis=1)
    base = jnp.sum(
        jnp.where(chunk[None] == jnp.arange(len(CHUNKS) + 1)[:, None, None], bases[:, None], 0), axis=0
    )

    def own(values):
        return lax.dynamic_index_in_dim(values, vir, axis=values.ndim - 1, keepdims=False)

    group_from, count_before = own(group_from), own(before(count.T).T)
    row_label = lax.dynamic_slice_in_dim(labels, vir * rows, rows, 0)
    row_rank = lax.dynamic_slice_in_dim(rank, vir * rows, rows, 0)
    row_member = row_label[None, :] == names[:, None]
    row_slot = row_rank + jnp.sum(
        jnp.where(row_member, (GROUP * group_from - count_before)[:, None], 0), axis=0
    )
    hit = jnp.arange(most * GROUP)[:, None] == row_slot[None, :]
    orbital = jnp.sum(jnp.where(hit, jnp.arange(rows)[None, :] + 1, 0), axis=1) - 1
    return dict(
        key=(labels * STRIDE + rank).reshape(1, total),
        pieces=pieces.reshape(-1),
        piece_from=piece_from.reshape(-1),
        piece_to=piece_to.reshape(-1),
        slot=slot.reshape(shards, 1, shard),
        label=own(group_label),
        tiles=own(group_tiles),
        depth=own(group_depth),
        unit=own(group_unit - base),
        chunk=own(chunk),
        label_end=own(label_end),
        label_turn=own(label_turn),
        starts=own(starts),
        head=own(jnp.stack([starts[0], starts[-3]])),
        tail=own(jnp.stack([starts[-3], starts[-1]])),
        clamped=jnp.maximum(orbital, 0),
        orbital=orbital.reshape(1, most * GROUP),
        overflow=overflow,
    )


def place_of(span, step, spare):
    return jnp.where(span[1] > span[0], jnp.minimum(span[0] + step, span[1] - 1), spare)


def compact_kernel(span, label, unit, tiles, depth, orbital, key_ref, *refs):
    slabs = refs[:GROUP]
    out_ref, onehot, held, product, stage, sem = refs[-6:]
    step = pl.program_id(0)
    last = pl.num_programs(0) - 1
    i = place_of(span, step, label.shape[0] - 1)
    na, _, nc, width = slabs[0].shape
    rows = na * nc
    slot = lax.rem(step, 2)
    deep, name = depth[i], label[i]

    def active(step):
        return span[0] + step < span[1]

    @pl.when(active(step) & ((step == 0) | (label[jnp.maximum(i - 1, 0)] != name)))
    def _():
        def build(k, carry):
            place = lax.broadcasted_iota(jnp.int32, (2 * TILE, width), 0)
            place = place + (name * STRIDE + k * 2 * TILE)
            onehot[k] = (key_ref[...] == place).astype(jnp.float32).astype(jnp.bfloat16)
            return carry

        lax.fori_loop(0, (deep + 1) // 2, build, 0)

    def copy(step, s):
        j = place_of(span, step, label.shape[0] - 1)
        size = tiles[j] * depth[j]
        return pltpu.make_async_copy(
            stage.at[s, pl.ds(0, size)], out_ref.at[pl.ds(unit[j], size)], sem.at[s]
        )

    @pl.when((step >= 2) & active(step - 2))
    def _():
        copy(step - 2, slot).wait()

    @pl.when(active(step))
    def _():
        for r in range(GROUP):
            held[r * rows : (r + 1) * rows, :] = slabs[r][...].reshape(rows, width)

        def part(k, carry):
            full = lax.dot_general(
                held[...], onehot[k], (((1,), (1,)), ((), ())), preferred_element_type=jnp.float32
            )
            for h in range(2):
                product[h] = full[:, h * TILE : (h + 1) * TILE]
            for h in range(2):

                @pl.when(2 * k + h < deep)
                def _():
                    for c in range(nc):
                        one = product[h, pl.ds(c, GROUP * na, stride=nc), :].astype(jnp.bfloat16)
                        for r in range(TILES):
                            stage[slot, r * deep + 2 * k + h, c] = one[
                                r * RUN * na : (r + 1) * RUN * na
                            ]

            return carry

        lax.fori_loop(0, (deep + 1) // 2, part, 0)
        copy(step, slot).start()

    @pl.when((step == last) & (step >= 1) & active(step - 1))
    def _():
        copy(step - 1, 1 - slot).wait()

    @pl.when((step == last) & active(step))
    def _():
        copy(step, slot).wait()


def token(*arrays):
    def kernel(*refs):
        refs[-1][...] = jnp.zeros_like(refs[-1])

    return pl.pallas_call(
        kernel,
        in_specs=[pl.BlockSpec(memory_space=pl.ANY)] * len(arrays),
        out_shape=jax.ShapeDtypeStruct((8, TILE), jnp.float32),
        cost_estimate=COST,
        name="token",
    )(*arrays)


def unset(shape, *marks):
    def kernel(*refs):
        del refs

    return pl.pallas_call(
        kernel,
        in_specs=[pl.BlockSpec(memory_space=pl.ANY)] * len(marks),
        out_specs=pl.BlockSpec(memory_space=pl.ANY),
        out_shape=jax.ShapeDtypeStruct(shape, jnp.bfloat16),
        cost_estimate=COST,
        name="unset",
    )(*marks)


def after(array, mark):
    def kernel(*refs):
        del refs

    return pl.pallas_call(
        kernel,
        in_specs=[pl.BlockSpec(memory_space=pl.ANY)] * 2,
        out_specs=pl.BlockSpec(memory_space=pl.ANY),
        out_shape=jax.ShapeDtypeStruct(array.shape, array.dtype),
        input_output_aliases={0: 0},
        cost_estimate=COST,
        name="after",
    )(array, mark)


def compact(integrals, plan, span, size, steps, pairs, first):
    na, rows, nc, width = integrals.shape
    spare = plan["label"].shape[0] - 1

    def slab(r):
        def at(step, span, label, unit, tiles, depth, orbital):
            return 0, orbital[place_of(span, step, spare) * GROUP + r], 0, 0

        return pl.BlockSpec((na, 1, nc, width), at)

    return pl.pallas_call(
        compact_kernel,
        grid_spec=pltpu.PrefetchScalarGridSpec(
            num_scalar_prefetch=6,
            grid=(steps,),
            in_specs=[pl.BlockSpec((1, width), lambda step, *_: (0, 0))]
            + [slab(r) for r in range(GROUP)]
            + [pl.BlockSpec(memory_space=pl.ANY)] * len(first),
            out_specs=pl.BlockSpec(memory_space=pl.ANY),
            scratch_shapes=[
                pltpu.VMEM((pairs, 2 * TILE, width), jnp.bfloat16),
                pltpu.VMEM((GROUP * na * nc, width), jnp.bfloat16),
                pltpu.VMEM((2, GROUP * na * nc, TILE), jnp.float32),
                pltpu.VMEM((2, TILES * 2 * pairs, nc, RUN * na, TILE), jnp.bfloat16),
                pltpu.SemaphoreType.DMA((2,)),
            ],
        ),
        out_shape=jax.ShapeDtypeStruct((size, nc, RUN * na, TILE), jnp.bfloat16),
        compiler_params=pltpu.CompilerParams(vmem_limit_bytes=VMEM),
        cost_estimate=COST,
        name="compact",
    )(
        span, plan["label"], plan["unit"], plan["tiles"], plan["depth"], plan["clamped"], plan["key"], *([integrals] * GROUP), *first,
    )


def fetch(buffers, source, row, v, c, held, sem, start):
    width = held.shape[0]
    for at in range(len(buffers)):

        @pl.when(source[v] == at)
        def _():
            rows = pl.ds(pl.multiple_of(row[v], width), width)
            copy = pltpu.make_async_copy(buffers[at].at[c, rows], held, sem)
            if start:
                copy.start()
            else:
                copy.wait()


def selection(slot, slots):
    width = slot.shape[-1]
    place = lax.broadcasted_iota(jnp.int32, (slots, width), 0)
    return (slot.reshape(1, width) == place).astype(jnp.float32).astype(jnp.bfloat16)


def add_kernel(nbuf, low, order, source, row, pieces, piece_from, piece_to, slot_ref, *refs):
    buffers = refs[:nbuf]
    out_ref, held, old, moved, sem, in_sem, out_sem = refs[-7:]
    shards = order.shape[0]
    step = pl.program_id(0)
    steps = pl.num_programs(0)
    nc = old.shape[0]
    slots = old.shape[1] * PIECE
    s = lax.rem(step, 2)

    def get(step, start):
        for c in range(nc):
            h = lax.rem(step, 2)
            fetch(buffers, source, row, order[low + step], c, held.at[h, c], sem.at[h, c], start)

    def each(v, c, do):
        for g in range(LABELS):
            size = pieces[g * shards + v]
            here = old.at[c, pl.ds(piece_from[g * shards + v], size)]
            there = out_ref.at[g, c, pl.ds(piece_to[g * shards + v], size)]

            @pl.when(size > 0)
            def _():
                do(g, here, there)

    v = order[low + step]

    @pl.when(step == 0)
    def _():
        get(step, True)

    @pl.when(step + 1 < steps)
    def _():
        get(step + 1, True)

    for c in range(nc):
        each(v, c, lambda g, here, there: pltpu.make_async_copy(there, here, in_sem.at[c, g]).start())
    onehot = selection(slot_ref[...], slots)
    get(step, False)
    for c in range(nc):
        sorted_rows = jnp.dot(onehot, held[s, c], preferred_element_type=jnp.float32)
        moved[...] = sorted_rows.astype(jnp.bfloat16).reshape(moved.shape)
        each(v, c, lambda g, here, there: pltpu.make_async_copy(there, here, in_sem.at[c, g]).wait())
        old[c] = old[c] + moved[...]
        each(v, c, lambda g, here, there: pltpu.make_async_copy(here, there, out_sem.at[c, g]).start())
    for c in range(nc):
        each(v, c, lambda g, here, there: pltpu.make_async_copy(here, there, out_sem.at[c, g]).wait())


def add_shards(ordered, buffers, places, low, high, plan, first=()):
    source, row, order = places
    nc, _, pairs = buffers[0].shape
    shards, _, shard = plan["slot"].shape
    slots = slots_of(shard)
    return pl.pallas_call(
        functools.partial(add_kernel, len(buffers), low),
        grid_spec=pltpu.PrefetchScalarGridSpec(
            num_scalar_prefetch=6,
            grid=(high - low,),
            in_specs=[
                pl.BlockSpec((1, 1, shard), lambda step, order, *_: (order[low + step], 0, 0))
            ]
            + [pl.BlockSpec(memory_space=pl.ANY)] * (len(buffers) + 1 + len(first)),
            out_specs=pl.BlockSpec(memory_space=pl.ANY),
            scratch_shapes=[
                pltpu.VMEM((2, nc, shard, pairs), jnp.bfloat16),
                pltpu.VMEM((nc, slots // PIECE, PIECE, pairs), jnp.bfloat16),
                pltpu.VMEM((slots // PIECE, PIECE, pairs), jnp.bfloat16),
                pltpu.SemaphoreType.DMA((2, nc)),
                pltpu.SemaphoreType.DMA((nc, LABELS)),
                pltpu.SemaphoreType.DMA((nc, LABELS)),
            ],
        ),
        out_shape=jax.ShapeDtypeStruct(ordered.shape, ordered.dtype),
        input_output_aliases={7 + len(buffers): 0},
        compiler_params=pltpu.CompilerParams(vmem_limit_bytes=VMEM),
        cost_estimate=COST,
        name="add_shards",
    )(
        order, source, row, plan["pieces"], plan["piece_from"], plan["piece_to"], plan["slot"], *buffers, ordered, *first,
    )


def multiply_kernel(low, high, span, label, unit, tiles, depth, label_end, label_turn, chunk, origin, *refs):
    count = 4 * (high - low)
    sources, amp_ref = refs[:count], refs[count]
    out_ref, total_ref, held, amp, held_sem, amp_sem = refs[-6:]
    step = pl.program_id(0)
    spare = label.shape[0] - 1
    i = place_of(span, step, spare)
    _, nc, rows, _ = sources[0].shape
    na = rows // RUN
    columns = total_ref.shape[0]
    count, deep = tiles[i], depth[i]
    slot, side = lax.rem(step, 2), lax.rem(label_turn[i], 2)
    follows = label_end[i]

    def get_units(step, start):
        j = place_of(span, step, spare)
        size, s = tiles[j] * depth[j], lax.rem(step, 2)
        for here in range(low, high):

            @pl.when(chunk[j] == here)
            def _():
                for at in range(4):
                    source = sources[4 * (here - low) + at]
                    copy = pltpu.make_async_copy(
                        source.at[pl.ds(unit[j], size)], held.at[s, at, pl.ds(0, size)], held_sem.at[s, at]
                    )
                    copy.start() if start else copy.wait()

    def get_amp(j, start):
        size, s = depth[j] * (TILE // PIECE), lax.rem(label_turn[j], 2)
        for c in range(nc):
            copy = pltpu.make_async_copy(
                amp_ref.at[label[j], c, pl.ds(0, size)], amp.at[s, c, pl.ds(0, size)], amp_sem.at[s, c]
            )
            copy.start() if start else copy.wait()

    active = span[0] + step < span[1]
    opens = active & ((step == 0) | (label[jnp.maximum(i - 1, 0)] != label[i]))

    @pl.when(active & (step == 0))
    def _():
        get_amp(i, True)
        get_units(step, True)

    @pl.when(span[0] + step + 1 < span[1])
    def _():
        get_units(step + 1, True)

    @pl.when(opens & (follows < span[1]))
    def _():
        get_amp(follows, True)

    @pl.when(active)
    def _():
        get_units(step, False)

    @pl.when(opens)
    def _():
        get_amp(i, False)

    def left(c, known):
        parts = []
        for s in range(4):
            for r in range(TILES):
                at = jnp.minimum(r, count - 1) * deep
                parts.append(jnp.concatenate([held[slot, s, at + k, c] for k in range(known)], axis=1))
        return jnp.concatenate(parts, axis=0)

    pieces, _, pairs = amp.shape[2:]
    for known in range(1, pieces * PIECE // TILE + 1):

        @pl.when(active & (deep == known))
        def _():
            lhs = jnp.concatenate([left(c, known) for c in range(nc)], axis=1)
            here = known * TILE // PIECE
            rhs = jnp.concatenate(
                [amp[side, c, :here].reshape(known * TILE, pairs) for c in range(nc)], axis=0
            )
            total = jnp.dot(lhs, rhs, preferred_element_type=jnp.float32)
            for j in range(columns):
                total_ref[j] = total[:, j * TILE : (j + 1) * TILE]

    @pl.when(active)
    def _():
        for s in range(4):
            for a in range(na):
                for j in range(columns):
                    picked = total_ref[j, pl.ds(s * TILES * rows + a, GROUP, stride=na), :]
                    out_ref[(origin[0] ^ s) * na + a, 0, :, j * TILE : (j + 1) * TILE] = (
                        picked.astype(jnp.bfloat16)
                    )


def multiply(sources, amplitudes, plan, origin, span, low, high, steps, done):
    _, nc, rows, _ = sources[0].shape
    _, _, pieces, piece, pairs = amplitudes.shape
    na = rows // RUN
    window = TILES * pieces * piece // TILE
    most = plan["label"].shape[0]
    spare = most - 1
    out_spec = pl.BlockSpec(
        (4 * na, 1, GROUP, pairs), lambda step, span, *_: (0, place_of(span, step, spare), 0, 0)
    )
    extra = [] if done is None else [done]
    return pl.pallas_call(
        functools.partial(multiply_kernel, low, high),
        grid_spec=pltpu.PrefetchScalarGridSpec(
            num_scalar_prefetch=9,
            grid=(steps,),
            in_specs=[pl.BlockSpec(memory_space=pl.ANY)] * (len(sources) + 1 + len(extra)),
            out_specs=out_spec,
            scratch_shapes=[
                pltpu.VMEM((pairs // TILE, 4 * TILES * rows, TILE), jnp.float32),
                pltpu.VMEM((2, 4, window, nc, rows, TILE), jnp.bfloat16),
                pltpu.VMEM((2, nc, pieces, piece, pairs), jnp.bfloat16),
                pltpu.SemaphoreType.DMA((2, 4)),
                pltpu.SemaphoreType.DMA((2, nc)),
            ],
        ),
        out_shape=jax.ShapeDtypeStruct((4 * na, most, GROUP, pairs), jnp.bfloat16),
        input_output_aliases={10 + len(sources): 0} if extra else {},
        compiler_params=pltpu.CompilerParams(vmem_limit_bytes=VMEM),
        cost_estimate=COST,
        name="multiply",
    )(
        span, plan["label"], plan["unit"],
        plan["tiles"], plan["depth"], plan["label_end"], plan["label_turn"], plan["chunk"], origin,
        *sources, amplitudes, *extra,
    )


def restore_kernel(live, orbital_ref, in_ref, out_ref, onehot, held):
    slots = orbital_ref.shape[1]
    rows, pairs = out_ref.shape[1:]

    @pl.when(pl.program_id(0) == 0)
    def _():
        place = lax.broadcasted_iota(jnp.int32, (rows, slots), 0)
        onehot[...] = (orbital_ref[...] == place).astype(jnp.float32).astype(jnp.bfloat16)

    sure = rows // GROUP
    for a in range(in_ref.shape[0]):
        for g in range(sure, in_ref.shape[1]):
            kept = jnp.where(g < live[0], in_ref[a, g], jnp.zeros_like(in_ref[a, g]))
            held[a, (g - sure) * GROUP : (g - sure + 1) * GROUP] = kept
        every = jnp.concatenate([in_ref[a, :sure].reshape(rows, pairs), held[a]], axis=0)
        out_ref[a] = jnp.dot(onehot[...], every, preferred_element_type=jnp.float32).astype(jnp.bfloat16)


def restore(grouped, plan, rows):
    block_a, most, _, pairs = grouped.shape
    return pl.pallas_call(
        restore_kernel,
        grid_spec=pltpu.PrefetchScalarGridSpec(
            num_scalar_prefetch=1,
            grid=(block_a // 4,),
            in_specs=[
                pl.BlockSpec((1, most * GROUP), lambda a, *_: (0, 0)),
                pl.BlockSpec((4, most, GROUP, pairs), lambda a, *_: (a, 0, 0, 0)),
            ],
            out_specs=pl.BlockSpec((4, rows, pairs), lambda a, *_: (a, 0, 0)),
            scratch_shapes=[
                pltpu.VMEM((rows, most * GROUP), jnp.bfloat16),
                pltpu.VMEM((4, (most - rows // GROUP) * GROUP, pairs), jnp.bfloat16),
            ],
        ),
        out_shape=jax.ShapeDtypeStruct((block_a, rows, pairs), jnp.bfloat16),
        compiler_params=pltpu.CompilerParams(vmem_limit_bytes=VMEM),
        cost_estimate=COST,
        name="restore",
    )(plan["starts"][-1:], plan["orbital"], grouped)


ORDER = (
    ((-1, 1), (1, 1), (1, 1), (1, 1)),
    ((-1, 2), (-1, 1), (-1, 1), (1, 2)),
    ((-1, 3), (-1, 2), (1, 2), (1, 3)),
)


class Gather:
    def __init__(self, amplitudes, vir, count):
        self.vir, self.count, self.lines = vir, count, count // 2
        self.ups, self.downs, self.across, self.sent = [amplitudes], [amplitudes], [], []

    def step(self, k, tied):
        count, lines, line = self.count, self.lines, self.vir // 2
        new = []
        if k == 0:
            send = self.ups[0]
        else:
            picks = ORDER[k - 1]
            send = self.pick(line, picks)
        if k > 0:
            send = tied(send)
        self.across.append(lax.ppermute(send, "vir", [(i, i ^ 1) for i in range(count)]))
        new.append(self.across[-1])
        if k < lines - 1:
            if k > 0:
                self.ups[k], self.downs[k] = tied(self.ups[k]), tied(self.downs[k])
            up, down = self.ups[k], self.downs[k]
            self.ups.append(lax.ppermute(up, "vir", [(i, i + 2) for i in range(2 * k, count - 2)]))
            self.downs.append(lax.ppermute(down, "vir", [(i, i - 2) for i in range(2, count - 2 * k)]))
            new += [self.ups[-1], self.downs[-1]]
        return new

    def pick(self, line, picks):
        kinds = [self.ups[hop] if way > 0 else self.downs[hop] for way, hop in picks]
        chosen = kinds[0]
        for at in range(1, self.lines):
            if kinds[at] is not kinds[at - 1]:
                chosen = jnp.where(line >= at, kinds[at], chosen)
        return chosen

    def places(self):
        lines, line, count = self.lines, self.vir // 2, self.count
        shards = jnp.arange(count, dtype=jnp.int32)
        ahead = shards // 2 - line
        same = jnp.where(ahead == 0, 0, jnp.where(ahead < 0, -ahead, lines - 1 + ahead))
        turn = jnp.zeros_like(shards)
        for k, picks in enumerate(ORDER):
            for at, (way, hop) in enumerate(picks):
                turn = jnp.where((line == at) & (ahead == -way * hop), k + 1, turn)
        own = shards % 2 == self.vir % 2
        source = jnp.where(own, same, 2 * lines - 1 + turn).astype(jnp.int32)
        step = jnp.where(own, jnp.abs(ahead), turn + 1) * count + shards
        place = jnp.sum((step[:, None] > step[None, :]).astype(jnp.int32), axis=1)
        order = jnp.sum(jnp.where(place[:, None] == shards[None, :], shards[:, None], 0), axis=0)
        return source, jnp.zeros((count,), jnp.int32), order.astype(jnp.int32)

    def buffers(self, k):
        hops = min(k, self.lines - 1)
        blank = [self.ups[0]] * (self.lines - 1 - hops)
        ways = self.ups[: hops + 1] + blank + self.downs[1 : hops + 1] + blank
        return ways + self.across[:k] + [self.ups[0]] * (self.lines - k)


class GatherWhole:
    def __init__(self, amplitudes):
        self.whole = lax.all_gather(amplitudes, "vir", axis=1, tiled=True)

    def step(self, k, tied):
        return []

    def places(self):
        shards = jnp.arange(8, dtype=jnp.int32)
        return jnp.zeros_like(shards), shards * (self.whole.shape[1] // 8), shards

    def buffers(self, k):
        return [self.whole]


def on_device(vir_count, integrals, amplitudes, irrep_labels):
    rows = integrals.shape[1]
    total = irrep_labels.shape[0]
    deepest = -(-(total // 4) // TILE)
    vir, occ = lax.axis_index("vir"), lax.axis_index("occ")
    plan = make_plan(irrep_labels, rows, vir, total // 8)
    most = ((rows // RUN + LABELS) * deepest, rows // GROUP + LABELS)
    core = [(i, i ^ 1) for i in range(4)]
    chip = [(i, i ^ 2) for i in range(4)]

    gather = Gather(amplitudes, vir, vir_count) if vir_count == 8 else GatherWhole(amplitudes)
    pairs = -(-deepest // 2)
    last = len(CHUNKS) - 1
    units, near, far, corner = [], [], [], []
    marks = [None]
    places = gather.places()
    pieces = deepest * TILE // PIECE
    ordered = jnp.zeros(
        (LABELS, amplitudes.shape[0], pieces, PIECE, amplitudes.shape[2]), jnp.bfloat16
    )
    come = (0, 1, 2, 7, 8)

    def tied(array):
        return after(array, marks[-1])

    def packed(at):
        span = plan["starts"][at : at + 2]
        return compact(integrals, plan, span, *CHUNKS[at], pairs, marks[-1:] if at > 1 else [])

    def exchange(at, units):
        return lax.ppermute(units, "occ", chip), lax.ppermute(units, "occ", core)

    units.append(packed(0))
    for k in range(last):
        new = gather.step(k, tied)
        if k > 0:
            units[k] = tied(units[k])
        ahead, beside = exchange(k, units[k])
        far.append(ahead)
        near.append(beside)
        if k > 0:
            far[k - 1] = after(far[k - 1], token(beside, marks[-1]))
            corner.append(lax.ppermute(far[k - 1], "occ", core))
            new.append(corner[-1])
        units.append(packed(k + 1))
        if k > 0:
            ordered = add_shards(
                ordered, gather.buffers(k), places, come[k - 1], come[k], plan, (marks[-1], units[-1])
            )
            new.append(ordered)
        marks.append(token(*new, ahead, beside, units[-1]))

    origin = occ.astype(jnp.int32).reshape(1)
    before = gather.buffers(last)
    gather.step(last, tied)
    ahead, beside = exchange(last, units[last])
    far.append(ahead)
    near.append(beside)
    corner.append(lax.ppermute(far[last - 1], "occ", core))
    ordered = add_shards(ordered, before, places, come[last - 1], come[last], plan)

    def more(*buffers):
        own = compact(integrals, plan, plan["starts"][last + 1 :], *most, pairs, [])
        ahead, beside = exchange(last + 1, own)
        return own, beside, ahead, lax.ppermute(ahead, "occ", core)

    shape = (most[0], *units[0].shape[1:])
    extra = unset(shape, token(ordered)), unset(shape), unset(shape), unset(shape)
    extra = lax.cond(plan["overflow"], more, lambda *buffers: buffers, *extra)
    ordered = add_shards(ordered, gather.buffers(last + 1), places, come[last], come[last + 1], plan)
    sources = [one for at in range(last) for one in (units[at], near[at], far[at], corner[at])]
    steps = min(sum(steps for _, steps in CHUNKS[:last]), rows // GROUP + LABELS)
    done = multiply(sources, ordered, plan, origin, plan["head"], 0, last, steps, None)
    far[last] = after(far[last], token(done))
    corner.append(lax.ppermute(far[last], "occ", core))
    sources = (units[last], near[last], far[last], corner[last], *extra)
    done = multiply(sources, ordered, plan, origin, plan["tail"], last, last + 2, most[1], done)
    return restore(done, plan, rows)


def solution(mesh):
    in_specs = (P("occ", "vir", None, None), P(None, "vir", "occ"), P())
    out_specs = P(None, "vir", "occ")
    return jax.shard_map(
        functools.partial(on_device, mesh.shape["vir"]),
        mesh=mesh, in_specs=in_specs, out_specs=out_specs, check_vma=False,
    )
```

profile of v0, /device:TPU:17, one launch (start us, length us, event | category | flops | bytes accessed | tf_op | source)
XLA Modules:
  0.0 280.6 jit_solution(17034089000202229269)
XLA Ops:
  0.0 1.2 collective-permute-start.5
  1.2 2.1 collective-permute-start.4
  3.3 4.4 %collective-permute-start.3 = (bf16[4,384,512]{2,1,0:T(8,128)(2,1)}, bf16[4,384,512]{2,1,0:T(8,128)(2,1)}, u32[]{:S(2)}, u32[]{:S(2)}) collective-permute-start(bf16[4,384,512]{2,1,0:T(8,128)(2,1)} %refs_0_.15), channel_id=1, source_target_pairs={{0,2},{1,3},{2,4},{3,5},{4,6},{5,7},{8,10},{9,11},{10,12},{11,13},... | collective-permute-start | bytes 4718600 | tf_op jit(solution)/shard_map/ppermute | solution.py:591
  7.7 0.7 eq.198
  8.5 0.8 dynamic_slice.48
  9.2 1.1 convert_reduce_fusion
  10.9 0.9 fusion.2
  12.3 0.6 add_select_fusion
  12.9 0.7 select_reduce_fusion.1
  14.2 0.7 select_reduce_fusion.5
  16.3 0.7 slice_reduce_fusion
  17.4 0.6 broadcast_maximum_fusion
  18.0 0.7 multiply_add_fusion
  18.7 11.1 %compact.6.refs_0_ = bf16[56,4,16,128]{3,2,1,0:T(8,128)(2,1)} custom-call(s32[2]{0:T(128)} %get-tuple-element.108.span, s32[33]{0:T(128)S(1)} %get-tuple-element.132.label, s32[33]{0:T(128)S(1)} %fusion.34.unit, s32[33]{0:T(128)S(1)} %get-tuple-element.133.tiles, s32[33]{0:T(128)S(1)} %fusion.36.depth, s32[528]{0:T(1024)S(1)} %get-tuple-element.126.orbital, ...), custom_call_target="tpu_custom_call" | custom-call | flops 1000000 | bytes 1000000 | tf_op jit(solution)/shard_map/compact/pallas_call | solution.py:261
  29.9 1.6 collective-permute-start.7
  31.5 1.2 collective-permute-start.6
  32.7 21.8 %compact.7.refs_5_.refs_0_ = bf16[128,4,16,128]{3,2,1,0:T(8,128)(2,1)} custom-call(s32[2]{0:T(128)} %get-tuple-element.107.span, s32[33]{0:T(128)S(1)} %get-tuple-element.132.label, s32[33]{0:T(128)S(1)} %fusion.34.unit, s32[33]{0:T(128)S(1)} %get-tuple-element.133.tiles, s32[33]{0:T(128)S(1)} %fusion.36.depth, s32[528]{0:T(1024)S(1)} %get-tuple-element.126.orbital, ...), custom_call_target="tpu_custom_call" | custom-call | flops 1000000 | bytes 1000000 | tf_op jit(solution)/shard_map/compact/pallas_call | solution.py:261
  54.6 0.6 token_.7.refs_1_.refs_16_.refs_12_
  55.5 0.9 collective-permute-start.13
  56.4 2.7 broadcast_select_fusion.refs_0_
  59.1 4.7 %collective-permute-start.8 = (bf16[4,384,512]{2,1,0:T(8,128)(2,1)}, bf16[4,384,512]{2,1,0:T(8,128)(2,1)}, u32[]{:S(2)}, u32[]{:S(2)}) collective-permute-start(bf16[4,384,512]{2,1,0:T(8,128)(2,1)} %after.12), channel_id=1, source_target_pairs={{0,1},{1,0},{2,3},{3,2},{4,5},{5,4},{6,7},{7,6},{8,9},{9,8},{10,11... | collective-permute-start | bytes 4718600 | tf_op jit(solution)/shard_map/ppermute | solution.py:585
  63.9 1.9 collective-permute-start.9
  65.8 5.8 %collective-permute-start.10 = (bf16[4,384,512]{2,1,0:T(8,128)(2,1)}, bf16[4,384,512]{2,1,0:T(8,128)(2,1)}, u32[]{:S(2)}, u32[]{:S(2)}) collective-permute-start(bf16[4,384,512]{2,1,0:T(8,128)(2,1)} %after.14.refs_4_), channel_id=1, source_target_pairs={{2,0},{3,1},{4,2},{5,3},{10,8},{11,9},{12,10},{13,11},{18,16},{19,... | collective-permute-start | bytes 4718600 | tf_op jit(solution)/shard_map/ppermute | solution.py:592
  71.6 1.4 copy-done.1
  73.6 1.3 collective-permute-start.12
  74.9 0.6 reshape.404.pieces
  75.5 0.6 reshape.405.piece_from
  78.0 0.6 reshape_add_fusion.slot_ref
  78.6 21.4 %compact.8.refs_13_.refs_7_.refs_0_ = bf16[128,4,16,128]{3,2,1,0:T(8,128)(2,1)} custom-call(s32[2]{0:T(128)} %get-tuple-element.106.span, s32[33]{0:T(128)S(1)} %get-tuple-element.132.label, s32[33]{0:T(128)S(1)} %fusion.34.unit, s32[33]{0:T(128)S(1)} %get-tuple-element.133.tiles, s32[33]{0:T(128)S(1)} %fusion.36.depth, s32[528]{0:T(1024)S(1)} %get-tuple-element.126.orbital, ...), custom_call_target="tpu_custom_call" | custom-call | flops 1000000 | bytes 1000000 | tf_op jit(solution)/shard_map/compact/pallas_call | solution.py:261
  100.5 8.5 %broadcast_in_dim.300.refs_11_ = bf16[8,4,48,16,512]{4,3,2,1,0:T(8,128)(2,1)} broadcast(bf16[]{:T(256)} %constant.222.clone.1), dimensions={} | broadcast | bytes 25165826 | tf_op jit(solution)/shard_map/broadcast_in_dim | solution.py:659
  109.0 6.9 %add_shards.4.refs_4_.refs_11_ = bf16[8,4,48,16,512]{4,3,2,1,0:T(8,128)(2,1)} custom-call(s32[8]{0:T(128)} %select_reduce_fusion.16.order, s32[8]{0:T(128)} %compare_select_fusion.5.source, s32[8]{0:T(128)} %broadcast.779.row, s32[64]{0:T(128)} %reshape.404.pieces, s32[64]{0:T(128)} %reshape.405.piece_from, ...), custom_call_target="tpu_custom_call", output_to_operand_aliasing={{}: (18, {})} | custom-call | flops 1000000 | bytes 1000000 | tf_op jit(solution)/shard_map/add_shards/pallas_call | solution.py:361
  115.9 0.6 token_.9.refs_16_.refs_1_.refs_12_
  116.5 1.2 collective-permute-start.18
  117.7 2.8 select_select_fusion.1.refs_0_
  120.5 2.4 collective-permute-start.20
  122.9 1.4 copy-done.2
  124.3 0.6 token_.10.refs_1_
  124.9 0.8 collective-permute-start.17
  125.7 1.9 collective-permute-start.21
  127.5 18.1 %compact.9.refs_13_.refs_7_.refs_0_ = bf16[152,4,16,128]{3,2,1,0:T(8,128)(2,1)} custom-call(s32[2]{0:T(128)} %get-tuple-element.109.span, s32[33]{0:T(128)S(1)} %get-tuple-element.132.label, s32[33]{0:T(128)S(1)} %fusion.34.unit, s32[33]{0:T(128)S(1)} %get-tuple-element.133.tiles, s32[33]{0:T(128)S(1)} %fusion.36.depth, s32[528]{0:T(1024)S(1)} %get-tuple-element.126.orbital, ...), custom_call_target="tpu_custom_call" | custom-call | flops 1000000 | bytes 1000000 | tf_op jit(solution)/shard_map/compact/pallas_call | solution.py:261
  145.6 9.7 %collective-permute-done.20.refs_1_.refs_3_ = bf16[4,384,512]{2,1,0:T(8,128)(2,1)} collective-permute-done((bf16[4,384,512]{2,1,0:T(8,128)(2,1)}, bf16[4,384,512]{2,1,0:T(8,128)(2,1)}, u32[]{:S(2)}, u32[]{:S(2)}) %collective-permute-start.20) | collective-permute-done | bytes 1572896 | tf_op jit(solution)/shard_map/ppermute | solution.py:591
  155.6 7.9 %collective-permute-done.18.refs_5_.refs_10_ = bf16[128,4,16,128]{3,2,1,0:T(8,128)(2,1)} collective-permute-done((bf16[128,4,16,128]{3,2,1,0:T(8,128)(2,1)}, bf16[128,4,16,128]{3,2,1,0:T(8,128)(2,1)}, u32[]{:S(2)}, u32[]{:S(2)}) %collective-permute-start.18) | collective-permute-done | bytes 2097184 | tf_op jit(solution)/shard_map/ppermute | solution.py:672
  163.5 2.3 collective-permute-start.19
  165.8 7.0 %add_shards.5.refs_4_.refs_11_ = bf16[8,4,48,16,512]{4,3,2,1,0:T(8,128)(2,1)} custom-call(s32[8]{0:T(128)} %select_reduce_fusion.16.order, s32[8]{0:T(128)} %compare_select_fusion.5.source, s32[8]{0:T(128)} %broadcast.779.row, s32[64]{0:T(128)} %reshape.404.pieces, s32[64]{0:T(128)} %reshape.405.piece_from, ...), custom_call_target="tpu_custom_call", output_to_operand_aliasing={{}: (18, {})} | custom-call | flops 1000000 | bytes 1000000 | tf_op jit(solution)/shard_map/add_shards/pallas_call | solution.py:361
  172.8 3.4 %select_select_fusion.refs_0_ = bf16[4,384,512]{2,1,0:T(8,128)(2,1)} fusion(bf16[4,384,512]{2,1,0:T(8,128)(2,1)} %collective-permute-done.20.refs_1_.refs_3_, bf16[4,384,512]{2,1,0:T(8,128)(2,1)} %after.19.refs_2_, bf16[4,384,512]{2,1,0:T(8,128)(2,1)} %after.20.refs_5_, bf16[4,384,512]{2,1,0:T(8,128)(2,1)} %collective-permute-done.21.refs_2_.refs_6_, ...), kind=kLoop, calls=%fused_computation.1 | loop fusion | flops 2359296 | bytes 7864323 | tf_op jit(solution)/shard_map/jit(_where)/select_n | solution.py:601
  176.2 0.6 token_.11.refs_1_
  176.8 0.7 copy-done.19
  177.5 0.8 fusion.28.span
  178.2 1.2 fusion.39.chunk
  179.4 1.3 fusion.37
  180.7 21.9 %add_shards.6.refs_11_.refs_0_ = bf16[8,4,48,16,512]{4,3,2,1,0:T(8,128)(2,1)} custom-call(s32[8]{0:T(128)} %select_reduce_fusion.16.order, s32[8]{0:T(128)} %compare_select_fusion.5.source, s32[8]{0:T(128)} %broadcast.779.row, s32[64]{0:T(128)} %reshape.404.pieces, s32[64]{0:T(128)} %reshape.405.piece_from, ...), custom_call_target="tpu_custom_call", output_to_operand_aliasing={{}: (18, {})} | custom-call | flops 1000000 | bytes 1000000 | tf_op jit(solution)/shard_map/add_shards/pallas_call | solution.py:361
  202.6 0.6 token_.13.refs_0_
  203.2 9.9 %collective-permute-done.23.refs_10_ = bf16[4,384,512]{2,1,0:T(8,128)(2,1)} collective-permute-done((bf16[4,384,512]{2,1,0:T(8,128)(2,1)}, bf16[4,384,512]{2,1,0:T(8,128)(2,1)}, u32[]{:S(2)}, u32[]{:S(2)}) %collective-permute-start.23) | collective-permute-done | bytes 1572896 | tf_op jit(solution)/shard_map/ppermute | solution.py:585
  213.2 7.1 %add_shards.7.refs_12_.refs_8_ = bf16[8,4,48,16,512]{4,3,2,1,0:T(8,128)(2,1)} custom-call(s32[8]{0:T(128)} %select_reduce_fusion.16.order, s32[8]{0:T(128)} %compare_select_fusion.5.source, s32[8]{0:T(128)} %broadcast.779.row, s32[64]{0:T(128)} %reshape.404.pieces, s32[64]{0:T(128)} %reshape.405.piece_from, ...), custom_call_target="tpu_custom_call", output_to_operand_aliasing={{}: (18, {})} | custom-call | flops 1000000 | bytes 1000000 | tf_op jit(solution)/shard_map/add_shards/pallas_call | solution.py:361
  220.3 28.2 %multiply.4.refs_0_.refs_9_ = bf16[16,33,16,512]{3,2,1,0:T(8,128)(2,1)} custom-call(s32[2]{0:T(128)} %fusion.28.span, s32[33]{0:T(128)S(1)} %get-tuple-element.132.label, s32[33]{0:T(128)S(1)} %fusion.34.unit, s32[33]{0:T(128)S(1)} %get-tuple-element.133.tiles, s32[33]{0:T(128)S(1)} %fusion.36.depth, s32[33]{0:T(128)} %get-tuple-element.134.label_end, ...), custom_call_target="tpu_custom_call" | custom-call | flops 1000000 | bytes 1000000 | tf_op jit(solution)/shard_map/multiply/pallas_call | solution.py:494
  248.5 0.6 token_.12.refs_1_
  249.1 1.5 copy-done.3
  250.6 0.8 collective-permute-start.24
  252.0 0.7 subtract_reduce_fusion.1
  253.3 0.8 fusion.27.span
  254.1 0.6 sub.114.orbital_ref
  254.7 1.4 collective-permute-done.24.refs_3_
  256.1 14.4 %multiply.5.in_ref = bf16[16,33,16,512]{3,2,1,0:T(8,128)(2,1)} custom-call(s32[2]{0:T(128)} %fusion.27.span, s32[33]{0:T(128)S(1)} %get-tuple-element.132.label, s32[33]{0:T(128)S(1)} %fusion.34.unit, s32[33]{0:T(128)S(1)} %get-tuple-element.133.tiles, s32[33]{0:T(128)S(1)} %fusion.36.depth, ...), custom_call_target="tpu_custom_call", output_to_operand_aliasing={{}: (18, {})} | custom-call | flops 1000000 | bytes 1000000 | tf_op jit(solution)/shard_map/multiply/pallas_call | solution.py:494
  270.5 10.1 %restore.1 = bf16[16,384,512]{2,1,0:T(8,128)(2,1)} custom-call(s32[1]{0:T(128)} %bitcast.7.live, s32[1,528]{1,0:T(1,128)} %sub.114.orbital_ref, bf16[16,33,16,512]{3,2,1,0:T(8,128)(2,1)} %multiply.5.in_ref), custom_call_target="tpu_custom_call" | custom-call | flops 1000000 | bytes 1000000 | tf_op jit(solution)/shard_map/restore/pallas_call | solution.py:541
  (134 shorter events, 7.6 us)
Async XLA Ops:
  0.0 54.6 %collective-permute-start.5 = (bf16[4,384,512]{2,1,0:T(8,128)(2,1)}, bf16[4,384,512]{2,1,0:T(8,128)(2,1)}, u32[]{:S(2)}, u32[]{:S(2)}) collective-permute-start(bf16[4,384,512]{2,1,0:T(8,128)(2,1)} %refs_0_.15), channel_id=1, source_target_pairs={{0,1},{1,0},{2,3},{3,2},{4,5},{5,4},{6,7},{7,6},{8,9},{9,8},{10,11... | collective-permute-start | bytes 4718600 | tf_op jit(solution)/shard_map/ppermute | solution.py:585
  1.2 53.3 %collective-permute-start.4 = (bf16[4,384,512]{2,1,0:T(8,128)(2,1)}, bf16[4,384,512]{2,1,0:T(8,128)(2,1)}, u32[]{:S(2)}, u32[]{:S(2)}) collective-permute-start(bf16[4,384,512]{2,1,0:T(8,128)(2,1)} %refs_0_.15), channel_id=1, source_target_pairs={{2,0},{3,1},{4,2},{5,3},{6,4},{7,5},{10,8},{11,9},{12,10},{13,11},... | collective-permute-start | bytes 4718600 | tf_op jit(solution)/shard_map/ppermute | solution.py:592
  3.3 51.3 %collective-permute-start.3 = (bf16[4,384,512]{2,1,0:T(8,128)(2,1)}, bf16[4,384,512]{2,1,0:T(8,128)(2,1)}, u32[]{:S(2)}, u32[]{:S(2)}) collective-permute-start(bf16[4,384,512]{2,1,0:T(8,128)(2,1)} %refs_0_.15), channel_id=1, source_target_pairs={{0,2},{1,3},{2,4},{3,5},{4,6},{5,7},{8,10},{9,11},{10,12},{11,13},... | collective-permute-start | bytes 4718600 | tf_op jit(solution)/shard_map/ppermute | solution.py:591
  11.9 18.0 %copy-start.4 = (s32[24,128]{1,0:T(8,128)}, s32[24,128]{1,0:T(8,128)S(1)}, u32[]{:S(2)}) copy-start(s32[24,128]{1,0:T(8,128)S(1)} %fusion.2) | copy-start | bytes 36868
  12.2 17.7 %copy-start.7 = (s32[8,8]{1,0:T(8,128)}, s32[8,8]{1,0:T(8,128)S(1)}, u32[]{:S(2)}) copy-start(s32[8,8]{1,0:T(8,128)S(1)} %fusion.12) | copy-start | bytes 772
  12.3 17.6 %copy-start.11 = (s32[8,8]{1,0:T(8,128)}, s32[8,8]{1,0:T(8,128)S(1)}, u32[]{:S(2)}) copy-start(s32[8,8]{1,0:T(8,128)S(1)} %select_reduce_fusion.3) | copy-start | bytes 772
  13.7 16.2 %copy-start.13 = (s32[8]{0:T(128)}, s32[8]{0:T(128)S(1)}, u32[]{:S(2)}) copy-start(s32[8]{0:T(128)S(1)} %get-tuple-element.130) | copy-start | bytes 100
  15.5 0.6 copy-start.18
  15.7 14.2 %copy-start.20 = (s32[8]{0:T(128)}, s32[8]{0:T(128)S(1)}, u32[]{:S(2)}) copy-start(s32[8]{0:T(128)S(1)} %get-tuple-element.111) | copy-start | bytes 100
  16.1 13.8 %copy-start.9 = (s32[6,1]{1,0:T(8,128)}, s32[6,1]{1,0:T(8,128)S(1)}, u32[]{:S(2)}) copy-start(s32[6,1]{1,0:T(8,128)S(1)} %constant_dynamic-slice_fusion.10) | copy-start | bytes 76
  16.2 13.7 %copy-start.15 = (s32[33,8]{0,1:T(8,128)}, s32[33,8]{0,1:T(8,128)S(1)}, u32[]{:S(2)}) copy-start(s32[33,8]{0,1:T(8,128)S(1)} %convert_reduce_fusion.3) | copy-start | bytes 3172
  29.9 24.6 %collective-permute-start.7 = (bf16[56,4,16,128]{3,2,1,0:T(8,128)(2,1)}, bf16[56,4,16,128]{3,2,1,0:T(8,128)(2,1)}, u32[]{:S(2)}, u32[]{:S(2)}) collective-permute-start(bf16[56,4,16,128]{3,2,1,0:T(8,128)(2,1)} %compact.6.refs_0_), channel_id=1, source_target_pairs={{0,8},{8,0},{16,24},{24,16},{1,9},{9,1},{17,25},{25,17},{2,10},{10... | collective-permute-start | bytes 2752520 | tf_op jit(solution)/shard_map/ppermute | solution.py:672
  31.5 23.0 %collective-permute-start.6 = (bf16[56,4,16,128]{3,2,1,0:T(8,128)(2,1)}, bf16[56,4,16,128]{3,2,1,0:T(8,128)(2,1)}, u32[]{:S(2)}, u32[]{:S(2)}) collective-permute-start(bf16[56,4,16,128]{3,2,1,0:T(8,128)(2,1)} %compact.6.refs_0_), channel_id=1, source_target_pairs={{0,16},{8,24},{16,0},{24,8},{1,17},{9,25},{17,1},{25,9},{2,18},{10... | collective-permute-start | bytes 2752520 | tf_op jit(solution)/shard_map/ppermute | solution.py:672
  55.2 16.4 %collective-permute-start.11 = (bf16[128,4,16,128]{3,2,1,0:T(8,128)(2,1)}, bf16[128,4,16,128]{3,2,1,0:T(8,128)(2,1)S(1)}, u32[]{:S(2)}, u32[]{:S(2)}) collective-permute-start(bf16[128,4,16,128]{3,2,1,0:T(8,128)(2,1)} %after.15.refs_4_), channel_id=1, source_target_pairs={{0,8},{8,0},{16,24},{24,16},{1,9},{9,1},{17,25},{25,17},{2,10},{10... | collective-permute-start | bytes 6291464 | tf_op jit(solution)/shard_map/ppermute | solution.py:672
  55.5 60.4 %collective-permute-start.13 = (bf16[128,4,16,128]{3,2,1,0:T(8,128)(2,1)}, bf16[128,4,16,128]{3,2,1,0:T(8,128)(2,1)}, u32[]{:S(2)}, u32[]{:S(2)}) collective-permute-start(bf16[128,4,16,128]{3,2,1,0:T(8,128)(2,1)} %after.15.refs_4_), channel_id=1, source_target_pairs={{0,16},{8,24},{16,0},{24,8},{1,17},{9,25},{17,1},{25,9},{2,18},{10... | collective-permute-start | bytes 6291464 | tf_op jit(solution)/shard_map/ppermute | solution.py:672
  59.1 56.7 %collective-permute-start.8 = (bf16[4,384,512]{2,1,0:T(8,128)(2,1)}, bf16[4,384,512]{2,1,0:T(8,128)(2,1)}, u32[]{:S(2)}, u32[]{:S(2)}) collective-permute-start(bf16[4,384,512]{2,1,0:T(8,128)(2,1)} %after.12), channel_id=1, source_target_pairs={{0,1},{1,0},{2,3},{3,2},{4,5},{5,4},{6,7},{7,6},{8,9},{9,8},{10,11... | collective-permute-start | bytes 4718600 | tf_op jit(solution)/shard_map/ppermute | solution.py:585
  63.9 52.0 %collective-permute-start.9 = (bf16[4,384,512]{2,1,0:T(8,128)(2,1)}, bf16[4,384,512]{2,1,0:T(8,128)(2,1)}, u32[]{:S(2)}, u32[]{:S(2)}) collective-permute-start(bf16[4,384,512]{2,1,0:T(8,128)(2,1)} %after.13.refs_1_), channel_id=1, source_target_pairs={{2,4},{3,5},{4,6},{5,7},{10,12},{11,13},{12,14},{13,15},{18,20},{1... | collective-permute-start | bytes 4718600 | tf_op jit(solution)/shard_map/ppermute | solution.py:591
  65.8 9.1 %copy-start.8 = (s32[8,8]{1,0:T(8,128)S(1)}, s32[8,8]{1,0:T(8,128)}, u32[]{:S(2)}) copy-start(s32[8,8]{1,0:T(8,128)} %copy-done.7) | copy-start | bytes 772
  65.8 9.7 %copy-start.12 = (s32[8,8]{1,0:T(8,128)S(1)}, s32[8,8]{1,0:T(8,128)}, u32[]{:S(2)}) copy-start(s32[8,8]{1,0:T(8,128)} %copy-done.11) | copy-start | bytes 772
  65.8 10.3 %copy-start.17 = (s32[8,8]{1,0:T(8,128)S(1)}, s32[8,8]{1,0:T(8,128)}, u32[]{:S(2)}) copy-start(s32[8,8]{1,0:T(8,128)} %get-tuple-element.124) | copy-start | bytes 772
  65.8 12.2 %copy-start.5 = (s32[24,128]{1,0:T(8,128)S(1)}, s32[24,128]{1,0:T(8,128)}, u32[]{:S(2)}) copy-start(s32[24,128]{1,0:T(8,128)} %copy-done.4) | copy-start | bytes 36868
  65.8 12.2 %copy-start.6 = (s32[8,384]{1,0:T(8,128)S(1)}, s32[8,384]{1,0:T(8,128)}, u32[]{:S(2)}) copy-start(s32[8,384]{1,0:T(8,128)} %get-tuple-element.94) | copy-start | bytes 36868
  65.8 50.1 %collective-permute-start.10 = (bf16[4,384,512]{2,1,0:T(8,128)(2,1)}, bf16[4,384,512]{2,1,0:T(8,128)(2,1)}, u32[]{:S(2)}, u32[]{:S(2)}) collective-permute-start(bf16[4,384,512]{2,1,0:T(8,128)(2,1)} %after.14.refs_4_), channel_id=1, source_target_pairs={{2,0},{3,1},{4,2},{5,3},{10,8},{11,9},{12,10},{13,11},{18,16},{19,... | collective-permute-start | bytes 4718600 | tf_op jit(solution)/shard_map/ppermute | solution.py:592
  71.6 1.4 copy-start.1
  73.6 42.3 %collective-permute-start.12 = (bf16[56,4,16,128]{3,2,1,0:T(8,128)(2,1)}, bf16[56,4,16,128]{3,2,1,0:T(8,128)(2,1)}, u32[]{:S(2)}, u32[]{:S(2)}) collective-permute-start(bf16[56,4,16,128]{3,2,1,0:T(8,128)(2,1)} %after.16.refs_2_), channel_id=1, source_target_pairs={{0,8},{8,0},{16,24},{24,16},{1,9},{9,1},{17,25},{25,17},{2,10},{10... | collective-permute-start | bytes 2752520 | tf_op jit(solution)/shard_map/ppermute | solution.py:684
  116.5 6.4 %collective-permute-start.16 = (bf16[128,4,16,128]{3,2,1,0:T(8,128)(2,1)}, bf16[128,4,16,128]{3,2,1,0:T(8,128)(2,1)S(1)}, u32[]{:S(2)}, u32[]{:S(2)}) collective-permute-start(bf16[128,4,16,128]{3,2,1,0:T(8,128)(2,1)} %after.17.refs_8_), channel_id=1, source_target_pairs={{0,8},{8,0},{16,24},{24,16},{1,9},{9,1},{17,25},{25,17},{2,10},{10... | collective-permute-start | bytes 6291464 | tf_op jit(solution)/shard_map/ppermute | solution.py:672
  116.5 47.0 %collective-permute-start.18 = (bf16[128,4,16,128]{3,2,1,0:T(8,128)(2,1)}, bf16[128,4,16,128]{3,2,1,0:T(8,128)(2,1)}, u32[]{:S(2)}, u32[]{:S(2)}) collective-permute-start(bf16[128,4,16,128]{3,2,1,0:T(8,128)(2,1)} %after.17.refs_8_), channel_id=1, source_target_pairs={{0,16},{8,24},{16,0},{24,8},{1,17},{9,25},{17,1},{25,9},{2,18},{10... | collective-permute-start | bytes 6291464 | tf_op jit(solution)/shard_map/ppermute | solution.py:672
  120.5 34.8 %collective-permute-start.20 = (bf16[4,384,512]{2,1,0:T(8,128)(2,1)}, bf16[4,384,512]{2,1,0:T(8,128)(2,1)}, u32[]{:S(2)}, u32[]{:S(2)}) collective-permute-start(bf16[4,384,512]{2,1,0:T(8,128)(2,1)} %after.19.refs_2_), channel_id=1, source_target_pairs={{4,6},{5,7},{12,14},{13,15},{20,22},{21,23},{28,30},{29,31}} | collective-permute-start | bytes 4718600 | tf_op jit(solution)/shard_map/ppermute | solution.py:591
  122.9 1.4 copy-start.2
  124.9 51.3 %collective-permute-start.17 = (bf16[128,4,16,128]{3,2,1,0:T(8,128)(2,1)}, bf16[128,4,16,128]{3,2,1,0:T(8,128)(2,1)}, u32[]{:S(2)}, u32[]{:S(2)}) collective-permute-start(bf16[128,4,16,128]{3,2,1,0:T(8,128)(2,1)} %after.18.refs_6_), channel_id=1, source_target_pairs={{0,8},{8,0},{16,24},{24,16},{1,9},{9,1},{17,25},{25,17},{2,10},{10... | collective-permute-start | bytes 6291464 | tf_op jit(solution)/shard_map/ppermute | solution.py:684
  125.7 47.1 %collective-permute-start.21 = (bf16[4,384,512]{2,1,0:T(8,128)(2,1)}, bf16[4,384,512]{2,1,0:T(8,128)(2,1)}, u32[]{:S(2)}, u32[]{:S(2)}) collective-permute-start(bf16[4,384,512]{2,1,0:T(8,128)(2,1)} %after.20.refs_5_), channel_id=1, source_target_pairs={{2,0},{3,1},{10,8},{11,9},{18,16},{19,17},{26,24},{27,25}} | collective-permute-start | bytes 4718600 | tf_op jit(solution)/shard_map/ppermute | solution.py:592
  127.5 48.7 %collective-permute-start.22 = (bf16[4,384,512]{2,1,0:T(8,128)(2,1)}, bf16[4,384,512]{2,1,0:T(8,128)(2,1)}, u32[]{:S(2)}, u32[]{:S(2)}) collective-permute-start(bf16[4,384,512]{2,1,0:T(8,128)(2,1)} %after.21), channel_id=1, source_target_pairs={{0,1},{1,0},{2,3},{3,2},{4,5},{5,4},{6,7},{7,6},{8,9},{9,8},{10,11... | collective-permute-start | bytes 4718600 | tf_op jit(solution)/shard_map/ppermute | solution.py:585
  155.3 93.7 %collective-permute-start.15 = (bf16[152,4,16,128]{3,2,1,0:T(8,128)(2,1)}, bf16[152,4,16,128]{3,2,1,0:T(8,128)(2,1)S(1)}, u32[]{:S(2)}, u32[]{:S(2)}) collective-permute-start(bf16[152,4,16,128]{3,2,1,0:T(8,128)(2,1)} %compact.9.refs_13_.refs_7_.refs_0_), channel_id=1, source_target_pairs={{0,16},{8,24},{16,0},{24,8},{1,17},{9,25},{17,1},{25,9},{2,18},{10... | collective-permute-start | bytes 7471112 | tf_op jit(solution)/shard_map/ppermute | solution.py:672
  163.5 56.8 %collective-permute-start.19 = (bf16[128,4,16,128]{3,2,1,0:T(8,128)(2,1)}, bf16[128,4,16,128]{3,2,1,0:T(8,128)(2,1)}, u32[]{:S(2)}, u32[]{:S(2)}) collective-permute-start(bf16[128,4,16,128]{3,2,1,0:T(8,128)(2,1)} %collective-permute-done.18.refs_5_.refs_10_), channel_id=1, source_target_pairs={{0,8},{8,0},{16,24},{24,16},{1,9},{9,1},{17,25},{25,17},{2,10},{10... | collective-permute-start | bytes 6291464 | tf_op jit(solution)/shard_map/ppermute | solution.py:700
  176.8 0.7 copy-start.19
  176.8 36.3 %collective-permute-start.23 = (bf16[4,384,512]{2,1,0:T(8,128)(2,1)}, bf16[4,384,512]{2,1,0:T(8,128)(2,1)}, u32[]{:S(2)}, u32[]{:S(2)}) collective-permute-start(bf16[4,384,512]{2,1,0:T(8,128)(2,1)} %after.22), channel_id=1, source_target_pairs={{0,1},{1,0},{2,3},{3,2},{4,5},{5,4},{6,7},{7,6},{8,9},{9,8},{10,11... | collective-permute-start | bytes 4718600 | tf_op jit(solution)/shard_map/ppermute | solution.py:585
  180.7 74.0 %collective-permute-start.14 = (bf16[152,4,16,128]{3,2,1,0:T(8,128)(2,1)}, bf16[152,4,16,128]{3,2,1,0:T(8,128)(2,1)}, u32[]{:S(2)}, u32[]{:S(2)}) collective-permute-start(bf16[152,4,16,128]{3,2,1,0:T(8,128)(2,1)} %compact.9.refs_13_.refs_7_.refs_0_), channel_id=1, source_target_pairs={{0,8},{8,0},{16,24},{24,16},{1,9},{9,1},{17,25},{25,17},{2,10},{10... | collective-permute-start | bytes 7471112 | tf_op jit(solution)/shard_map/ppermute | solution.py:672
  249.1 2.3 copy-start.10
  249.1 2.9 %copy-start.14 = (s32[8]{0:T(128)S(1)}, s32[8]{0:T(128)}, u32[]{:S(2)}) copy-start(s32[8]{0:T(128)} %copy-done.13) | copy-start | bytes 100
  249.1 2.9 %copy-start.21 = (s32[8]{0:T(128)S(1)}, s32[8]{0:T(128)}, u32[]{:S(2)}) copy-start(s32[8]{0:T(128)} %copy-done.20) | copy-start | bytes 100
  249.1 5.0 %copy-start.16 = (s32[528]{0:T(1024)S(1)}, s32[528]{0:T(1024)}, u32[]{:S(2)}) copy-start(s32[528]{0:T(1024)} %get-tuple-element.127) | copy-start | bytes 6340
  249.1 1.5 copy-start.3
  250.6 5.5 %collective-permute-start.24 = (bf16[152,4,16,128]{3,2,1,0:T(8,128)(2,1)}, bf16[152,4,16,128]{3,2,1,0:T(8,128)(2,1)}, u32[]{:S(2)}, u32[]{:S(2)}) collective-permute-start(bf16[152,4,16,128]{3,2,1,0:T(8,128)(2,1)} %after.23.refs_2_), channel_id=1, source_target_pairs={{0,8},{8,0},{16,24},{24,16},{1,9},{9,1},{17,25},{25,17},{2,10},{10... | collective-permute-start | bytes 7471112 | tf_op jit(solution)/shard_map/ppermute | solution.py:716
where the time goes:
time: 282 us; the launch traced here: 281 us
  Pallas kernels  172 us (61%)
  starting transfers between devices  35 us (12%)
  waiting for transfers between devices  29.1 us (10%)
  local copies, waits for them, and re-layouts  24 us (9%)
  other arithmetic  18.2 us (6%)
    pallas_call x4, Pallas kernels, compact(): pl.pallas_call(compact_kernel, grid_spec=pltpu.PrefetchScalarGridSpec(num...  72.4 us
    pallas_call x4, Pallas kernels, add_shards(): pl.pallas_call(functools.partial(add_kernel, len(buffers), low), grid_spe...  42.9 us
    pallas_call x2, Pallas kernels, multiply(): pl.pallas_call(functools.partial(multiply_kernel, low, high), grid_spec=p...  42.6 us
    pallas_call x1, Pallas kernels, restore(): pl.pallas_call(restore_kernel, grid_spec=pltpu.PrefetchScalarGridSpec(num...  10.1 us
    ppermute x4, waiting for transfers between devices, step(): lax.ppermute(send, 'vir', [(i, i ^ 1) for i in range(count)])  9.94 us
    ppermute x3, waiting for transfers between devices, step(): lax.ppermute(up, 'vir', [(i, i + 2) for i in range(2 * k, count - 2)])  9.72 us
    ppermute x3, starting transfers between devices, step(): lax.ppermute(down, 'vir', [(i, i - 2) for i in range(2, count - 2 * k)])  9.68 us
    select_n x3, other arithmetic, pick(): chosen = jnp.where(line >= at, kinds[at], chosen)  8.87 us
  transfers between devices with their start and end apart: 22, of which 4 were waited for; matrix products, arithmetic and copies ran while one was open for 14% of the time, Pallas kernels for 52%

commit v1 on v0

--- a/solution.py
+++ b/solution.py
@@ -16,7 +16,7 @@
 STRIDE = 1024
 VMEM = 56 * 2**20
 COST = pl.CostEstimate(flops=10**6, bytes_accessed=10**6, transcendentals=0)
-CHUNKS = ((56, 6), (128, 12), (128, 12), (152, 18))
+CHUNKS = ((48, 5), (104, 10), (104, 10), (192, 20))
 
 
 def before(values):
@@ -659,7 +659,7 @@
     ordered = jnp.zeros(
         (LABELS, amplitudes.shape[0], pieces, PIECE, amplitudes.shape[2]), jnp.bfloat16
     )
-    come = (0, 1, 2, 7, 8)
+    come = (0, 1, 1, 7, 8)
 
     def tied(array):
         return after(array, marks[-1])
@@ -684,7 +684,7 @@
             corner.append(lax.ppermute(far[k - 1], "occ", core))
             new.append(corner[-1])
         units.append(packed(k + 1))
-        if k > 0:
+        if k > 0 and come[k] > come[k - 1]:
             ordered = add_shards(
                 ordered, gather.buffers(k), places, come[k - 1], come[k], plan, (marks[-1], units[-1])
             )

time: 282 us -> 262 us (0.929)
  waiting for transfers between devices: 29.1 us -> 15.4 us
    ppermute x3, waiting for transfers between devices: 9.72 us -> 2.59 us  [step(): lax.ppermute(up, 'vir', [(i, i + 2) for i in range(2 * k, count - 2)])]
    ppermute x4, waiting for transfers between devices: 9.94 us -> 5.74 us  [step(): lax.ppermute(send, 'vir', [(i, i ^ 1) for i in range(count)])]
    ppermute x8, waiting for transfers between devices: 7.96 us -> 4.66 us  [exchange(): return (lax.ppermute(units, 'occ', chip), lax.ppermute(units, 'occ', core))]
    pallas_call x4 -> x3, Pallas kernels: 42.9 us -> 39.9 us  [add_shards(): pl.pallas_call(functools.partial(add_kernel, len(buffers), low), grid_spe...]
  transfers between devices with their start and end apart: 22 -> 22, of which waited for: 4 -> 4; matrix products, arithmetic and copies ran while one was open for 14% -> 14% of each run, Pallas kernels for 52% -> 54%
where the time goes in v1:
time: 262 us
  Pallas kernels  170 us (65%)
  starting transfers between devices  33 us (13%)
  local copies, waits for them, and re-layouts  23.4 us (9%)
  other arithmetic  18.2 us (7%)
  waiting for transfers between devices  15.4 us (6%)
    pallas_call x4, Pallas kernels, compact(): pl.pallas_call(compact_kernel, grid_spec=pltpu.PrefetchScalarGridSpec(num...  74.7 us
    pallas_call x2, Pallas kernels, multiply(): pl.pallas_call(functools.partial(multiply_kernel, low, high), grid_spec=p...  40.8 us
    pallas_call x3, Pallas kernels, add_shards(): pl.pallas_call(functools.partial(add_kernel, len(buffers), low), grid_spe...  39.9 us
    pallas_call x1, Pallas kernels, restore(): pl.pallas_call(restore_kernel, grid_spec=pltpu.PrefetchScalarGridSpec(num...  10 us
    ppermute x3, starting transfers between devices, step(): lax.ppermute(down, 'vir', [(i, i - 2) for i in range(2, count - 2 * k)])  9.68 us
    select_n x3, other arithmetic, pick(): chosen = jnp.where(line >= at, kinds[at], chosen)  8.77 us
    ppermute x3, starting transfers between devices, step(): lax.ppermute(up, 'vir', [(i, i + 2) for i in range(2 * k, count - 2)])  8.7 us
    broadcast_in_dim x1, local copies, waits for them, and re-layouts, on_device(): jnp.zeros((LABELS, amplitudes.shape[0], pieces, PIECE, amplitudes.shape[2...  8.49 us
  transfers between devices with their start and end apart: 22, of which 4 were waited for; matrix products, arithmetic and copies ran while one was open for 14% of the time, Pallas kernels for 54%

profile of v1, /device:TPU:17, one launch (start us, length us, event | category | flops | bytes accessed | tf_op | source)
XLA Modules:
  0.0 261.7 jit_solution(1361853324200243584)
XLA Ops:
  0.0 1.2 collective-permute-start.5
  1.2 2.1 collective-permute-start.4
  3.3 4.4 %collective-permute-start.3 = (bf16[4,384,512]{2,1,0:T(8,128)(2,1)}, bf16[4,384,512]{2,1,0:T(8,128)(2,1)}, u32[]{:S(2)}, u32[]{:S(2)}) collective-permute-start(bf16[4,384,512]{2,1,0:T(8,128)(2,1)} %refs_0_.13), channel_id=1, source_target_pairs={{0,2},{1,3},{2,4},{3,5},{4,6},{5,7},{8,10},{9,11},{10,12},{11,13},... | collective-permute-start | bytes 4718600 | tf_op jit(solution)/shard_map/ppermute | solution.py:591
  7.7 0.7 eq.198
  8.4 0.8 dynamic_slice.48
  9.2 1.1 convert_reduce_fusion
  10.9 0.9 fusion.2
  12.3 0.6 add_select_fusion
  12.9 0.7 select_reduce_fusion.1
  14.2 0.7 select_reduce_fusion.5
  16.3 0.7 slice_reduce_fusion
  17.4 0.6 broadcast_maximum_fusion
  18.0 0.7 multiply_add_fusion
  18.7 10.4 %compact.6.refs_0_ = bf16[48,4,16,128]{3,2,1,0:T(8,128)(2,1)} custom-call(s32[2]{0:T(128)} %get-tuple-element.108.span, s32[33]{0:T(128)S(1)} %get-tuple-element.132.label, s32[33]{0:T(128)S(1)} %fusion.34.unit, s32[33]{0:T(128)S(1)} %get-tuple-element.133.tiles, s32[33]{0:T(128)S(1)} %fusion.36.depth, s32[528]{0:T(1024)S(1)} %get-tuple-element.126.orbital, ...), custom_call_target="tpu_custom_call" | custom-call | flops 1000000 | bytes 1000000 | tf_op jit(solution)/shard_map/compact/pallas_call | solution.py:261
  29.2 1.6 collective-permute-start.7
  30.8 1.2 collective-permute-start.6
  32.0 21.3 %compact.7.refs_5_.refs_0_ = bf16[104,4,16,128]{3,2,1,0:T(8,128)(2,1)} custom-call(s32[2]{0:T(128)} %get-tuple-element.107.span, s32[33]{0:T(128)S(1)} %get-tuple-element.132.label, s32[33]{0:T(128)S(1)} %fusion.34.unit, s32[33]{0:T(128)S(1)} %get-tuple-element.133.tiles, s32[33]{0:T(128)S(1)} %fusion.36.depth, s32[528]{0:T(1024)S(1)} %get-tuple-element.126.orbital, ...), custom_call_target="tpu_custom_call" | custom-call | flops 1000000 | bytes 1000000 | tf_op jit(solution)/shard_map/compact/pallas_call | solution.py:261
  53.4 0.6 token_.7.refs_1_.refs_16_.refs_12_
  54.6 2.7 %broadcast_select_fusion.refs_0_ = bf16[4,384,512]{2,1,0:T(8,128)(2,1)} fusion(bf16[4,384,512]{2,1,0:T(8,128)(2,1)} %collective-permute-done.3.refs_1_.refs_0_, bf16[4,384,512]{2,1,0:T(8,128)(2,1)} %collective-permute-done.4.refs_2_.refs_0_, pred[]{:T(512)S(6)} %ge.50), kind=kLoop, calls=%fused_computation.3 | loop fusion | flops 786432 | bytes 4718593 | tf_op jit(solution)/shard_map/jit(_where)/select_n | solution.py:601
  57.3 0.8 collective-permute-start.8
  58.1 1.9 collective-permute-start.9
  60.1 5.8 %collective-permute-start.10 = (bf16[4,384,512]{2,1,0:T(8,128)(2,1)}, bf16[4,384,512]{2,1,0:T(8,128)(2,1)}, u32[]{:S(2)}, u32[]{:S(2)}) collective-permute-start(bf16[4,384,512]{2,1,0:T(8,128)(2,1)} %after.14.refs_4_), channel_id=1, source_target_pairs={{2,0},{3,1},{4,2},{5,3},{10,8},{11,9},{12,10},{13,11},{18,16},{19,... | collective-permute-start | bytes 4718600 | tf_op jit(solution)/shard_map/ppermute | solution.py:592
  65.9 1.3 copy-done.2
  67.2 0.6 token_.8.refs_1_
  67.8 1.3 collective-permute-start.12
  69.1 0.6 reshape.404.pieces
  69.7 0.7 reshape.405.piece_from
  71.6 0.6 select_reduce_fusion.16.order
  72.3 0.6 reshape_add_fusion.slot_ref
  72.9 19.2 %compact.8.refs_13_.refs_7_.refs_0_ = bf16[104,4,16,128]{3,2,1,0:T(8,128)(2,1)} custom-call(s32[2]{0:T(128)} %get-tuple-element.106.span, s32[33]{0:T(128)S(1)} %get-tuple-element.132.label, s32[33]{0:T(128)S(1)} %fusion.34.unit, s32[33]{0:T(128)S(1)} %get-tuple-element.133.tiles, s32[33]{0:T(128)S(1)} %fusion.36.depth, s32[528]{0:T(1024)S(1)} %get-tuple-element.126.orbital, ...), custom_call_target="tpu_custom_call" | custom-call | flops 1000000 | bytes 1000000 | tf_op jit(solution)/shard_map/compact/pallas_call | solution.py:261
  92.6 8.5 %broadcast_in_dim.300.refs_11_ = bf16[8,4,48,16,512]{4,3,2,1,0:T(8,128)(2,1)} broadcast(bf16[]{:T(256)} %constant.223.clone.1), dimensions={} | broadcast | bytes 25165826 | tf_op jit(solution)/shard_map/broadcast_in_dim | solution.py:659
  101.1 6.9 %add_shards.3.refs_4_.refs_11_ = bf16[8,4,48,16,512]{4,3,2,1,0:T(8,128)(2,1)} custom-call(s32[8]{0:T(128)} %select_reduce_fusion.16.order, s32[8]{0:T(128)} %compare_select_fusion.5.source, s32[8]{0:T(128)} %broadcast.780.row, s32[64]{0:T(128)} %reshape.404.pieces, s32[64]{0:T(128)} %reshape.405.piece_from, ...), custom_call_target="tpu_custom_call", output_to_operand_aliasing={{}: (18, {})} | custom-call | flops 1000000 | bytes 1000000 | tf_op jit(solution)/shard_map/add_shards/pallas_call | solution.py:361
  108.0 0.6 token_.9.refs_16_.refs_1_
  108.6 2.8 %select_select_fusion.1.refs_0_ = bf16[4,384,512]{2,1,0:T(8,128)(2,1)} fusion(bf16[4,384,512]{2,1,0:T(8,128)(2,1)} %collective-permute-done.9.refs_1_.refs_0_, bf16[4,384,512]{2,1,0:T(8,128)(2,1)} %after.14.refs_4_, bf16[4,384,512]{2,1,0:T(8,128)(2,1)} %collective-permute-done.10.refs_2_.refs_0_, pred[]{:T(512)S(6)} %ge.51, pred[]{:T(512)S(6)} %ge.50), kind=kLoop, calls=%fused_computation.2 | loop fusion | flops 1572864 | bytes 6291458 | tf_op jit(solution)/shard_map/jit(_where)/select_n | solution.py:601
  111.4 2.4 collective-permute-start.20
  113.8 1.2 collective-permute-start.18
  115.0 1.8 collective-permute-start.21
  116.9 1.3 copy-done.1
  118.2 0.6 token_.10.refs_1_
  118.8 0.8 collective-permute-start.17
  119.5 0.6 collective-permute-start.22
  120.2 23.8 %compact.9.refs_6_.refs_0_ = bf16[192,4,16,128]{3,2,1,0:T(8,128)(2,1)} custom-call(s32[2]{0:T(128)} %get-tuple-element.109.span, s32[33]{0:T(128)S(1)} %get-tuple-element.132.label, s32[33]{0:T(128)S(1)} %fusion.34.unit, s32[33]{0:T(128)S(1)} %get-tuple-element.133.tiles, s32[33]{0:T(128)S(1)} %fusion.36.depth, s32[528]{0:T(1024)S(1)} %get-tuple-element.126.orbital, ...), custom_call_target="tpu_custom_call" | custom-call | flops 1000000 | bytes 1000000 | tf_op jit(solution)/shard_map/compact/pallas_call | solution.py:261
  143.9 2.6 collective-permute-done.20.refs_1_.refs_3_
  146.5 1.2 collective-permute-start.15
  147.8 4.6 %collective-permute-done.18.refs_4_.refs_10_ = bf16[104,4,16,128]{3,2,1,0:T(8,128)(2,1)} collective-permute-done((bf16[104,4,16,128]{3,2,1,0:T(8,128)(2,1)}, bf16[104,4,16,128]{3,2,1,0:T(8,128)(2,1)}, u32[]{:S(2)}, u32[]{:S(2)}) %collective-permute-start.18) | collective-permute-done | bytes 1703968 | tf_op jit(solution)/shard_map/ppermute | solution.py:672
  152.4 2.3 collective-permute-start.19
  154.7 3.3 %select_select_fusion.refs_0_ = bf16[4,384,512]{2,1,0:T(8,128)(2,1)} fusion(bf16[4,384,512]{2,1,0:T(8,128)(2,1)} %collective-permute-done.20.refs_1_.refs_3_, bf16[4,384,512]{2,1,0:T(8,128)(2,1)} %after.19.refs_2_, bf16[4,384,512]{2,1,0:T(8,128)(2,1)} %after.20.refs_5_, bf16[4,384,512]{2,1,0:T(8,128)(2,1)} %collective-permute-done.21.refs_2_.refs_6_, ...), kind=kLoop, calls=%fused_computation.1 | loop fusion | flops 2359296 | bytes 7864323 | tf_op jit(solution)/shard_map/jit(_where)/select_n | solution.py:601
  158.0 0.6 token_.11.refs_1_
  158.6 0.7 collective-permute-start.23
  159.3 0.7 fusion.28.span
  160.0 1.3 fusion.39.chunk
  161.3 1.3 fusion.37
  162.8 25.8 %add_shards.4.refs_11_.refs_0_ = bf16[8,4,48,16,512]{4,3,2,1,0:T(8,128)(2,1)} custom-call(s32[8]{0:T(128)} %select_reduce_fusion.16.order, s32[8]{0:T(128)} %compare_select_fusion.5.source, s32[8]{0:T(128)} %broadcast.780.row, s32[64]{0:T(128)} %reshape.404.pieces, s32[64]{0:T(128)} %reshape.405.piece_from, ...), custom_call_target="tpu_custom_call", output_to_operand_aliasing={{}: (18, {})} | custom-call | flops 1000000 | bytes 1000000 | tf_op jit(solution)/shard_map/add_shards/pallas_call | solution.py:361
  188.6 0.6 token_.13.refs_0_
  189.2 5.7 %collective-permute-done.23.refs_10_ = bf16[4,384,512]{2,1,0:T(8,128)(2,1)} collective-permute-done((bf16[4,384,512]{2,1,0:T(8,128)(2,1)}, bf16[4,384,512]{2,1,0:T(8,128)(2,1)}, u32[]{:S(2)}, u32[]{:S(2)}) %collective-permute-start.23) | collective-permute-done | bytes 1572896 | tf_op jit(solution)/shard_map/ppermute | solution.py:585
  195.0 7.2 %add_shards.5.refs_12_.refs_8_ = bf16[8,4,48,16,512]{4,3,2,1,0:T(8,128)(2,1)} custom-call(s32[8]{0:T(128)} %select_reduce_fusion.16.order, s32[8]{0:T(128)} %compare_select_fusion.5.source, s32[8]{0:T(128)} %broadcast.780.row, s32[64]{0:T(128)} %reshape.404.pieces, s32[64]{0:T(128)} %reshape.405.piece_from, ...), custom_call_target="tpu_custom_call", output_to_operand_aliasing={{}: (18, {})} | custom-call | flops 1000000 | bytes 1000000 | tf_op jit(solution)/shard_map/add_shards/pallas_call | solution.py:361
  202.2 24.2 %multiply.4.refs_0_.refs_9_ = bf16[16,33,16,512]{3,2,1,0:T(8,128)(2,1)} custom-call(s32[2]{0:T(128)} %fusion.28.span, s32[33]{0:T(128)S(1)} %get-tuple-element.132.label, s32[33]{0:T(128)S(1)} %fusion.34.unit, s32[33]{0:T(128)S(1)} %get-tuple-element.133.tiles, s32[33]{0:T(128)S(1)} %fusion.36.depth, s32[33]{0:T(128)} %get-tuple-element.134.label_end, ...), custom_call_target="tpu_custom_call" | custom-call | flops 1000000 | bytes 1000000 | tf_op jit(solution)/shard_map/multiply/pallas_call | solution.py:494
  227.0 1.6 copy-done.3
  228.7 0.8 collective-permute-start.24
  230.0 0.6 subtract_reduce_fusion.1
  231.3 0.8 fusion.27.span
  232.7 2.4 collective-permute-done.24.refs_3_
  235.1 16.6 %multiply.5.in_ref = bf16[16,33,16,512]{3,2,1,0:T(8,128)(2,1)} custom-call(s32[2]{0:T(128)} %fusion.27.span, s32[33]{0:T(128)S(1)} %get-tuple-element.132.label, s32[33]{0:T(128)S(1)} %fusion.34.unit, s32[33]{0:T(128)S(1)} %get-tuple-element.133.tiles, s32[33]{0:T(128)S(1)} %fusion.36.depth, ...), custom_call_target="tpu_custom_call", output_to_operand_aliasing={{}: (18, {})} | custom-call | flops 1000000 | bytes 1000000 | tf_op jit(solution)/shard_map/multiply/pallas_call | solution.py:494
  251.7 10.0 %restore.1 = bf16[16,384,512]{2,1,0:T(8,128)(2,1)} custom-call(s32[1]{0:T(128)} %bitcast.7.live, s32[1,528]{1,0:T(1,128)} %sub.114.orbital_ref, bf16[16,33,16,512]{3,2,1,0:T(8,128)(2,1)} %multiply.5.in_ref), custom_call_target="tpu_custom_call" | custom-call | flops 1000000 | bytes 1000000 | tf_op jit(solution)/shard_map/restore/pallas_call | solution.py:541
  (133 shorter events, 7.9 us)
Async XLA Ops:
  0.0 53.4 %collective-permute-start.5 = (bf16[4,384,512]{2,1,0:T(8,128)(2,1)}, bf16[4,384,512]{2,1,0:T(8,128)(2,1)}, u32[]{:S(2)}, u32[]{:S(2)}) collective-permute-start(bf16[4,384,512]{2,1,0:T(8,128)(2,1)} %refs_0_.13), channel_id=1, source_target_pairs={{0,1},{1,0},{2,3},{3,2},{4,5},{5,4},{6,7},{7,6},{8,9},{9,8},{10,11... | collective-permute-start | bytes 4718600 | tf_op jit(solution)/shard_map/ppermute | solution.py:585
  1.2 52.2 %collective-permute-start.4 = (bf16[4,384,512]{2,1,0:T(8,128)(2,1)}, bf16[4,384,512]{2,1,0:T(8,128)(2,1)}, u32[]{:S(2)}, u32[]{:S(2)}) collective-permute-start(bf16[4,384,512]{2,1,0:T(8,128)(2,1)} %refs_0_.13), channel_id=1, source_target_pairs={{2,0},{3,1},{4,2},{5,3},{6,4},{7,5},{10,8},{11,9},{12,10},{13,11},... | collective-permute-start | bytes 4718600 | tf_op jit(solution)/shard_map/ppermute | solution.py:592
  3.3 50.1 %collective-permute-start.3 = (bf16[4,384,512]{2,1,0:T(8,128)(2,1)}, bf16[4,384,512]{2,1,0:T(8,128)(2,1)}, u32[]{:S(2)}, u32[]{:S(2)}) collective-permute-start(bf16[4,384,512]{2,1,0:T(8,128)(2,1)} %refs_0_.13), channel_id=1, source_target_pairs={{0,2},{1,3},{2,4},{3,5},{4,6},{5,7},{8,10},{9,11},{10,12},{11,13},... | collective-permute-start | bytes 4718600 | tf_op jit(solution)/shard_map/ppermute | solution.py:591
  11.9 17.3 %copy-start.4 = (s32[24,128]{1,0:T(8,128)}, s32[24,128]{1,0:T(8,128)S(1)}, u32[]{:S(2)}) copy-start(s32[24,128]{1,0:T(8,128)S(1)} %fusion.2) | copy-start | bytes 36868
  12.2 17.0 %copy-start.7 = (s32[8,8]{1,0:T(8,128)}, s32[8,8]{1,0:T(8,128)S(1)}, u32[]{:S(2)}) copy-start(s32[8,8]{1,0:T(8,128)S(1)} %fusion.12) | copy-start | bytes 772
  12.3 16.9 %copy-start.11 = (s32[8,8]{1,0:T(8,128)}, s32[8,8]{1,0:T(8,128)S(1)}, u32[]{:S(2)}) copy-start(s32[8,8]{1,0:T(8,128)S(1)} %select_reduce_fusion.3) | copy-start | bytes 772
  13.7 15.5 %copy-start.13 = (s32[8]{0:T(128)}, s32[8]{0:T(128)S(1)}, u32[]{:S(2)}) copy-start(s32[8]{0:T(128)S(1)} %get-tuple-element.130) | copy-start | bytes 100
  15.5 0.6 copy-start.18
  15.7 13.5 %copy-start.20 = (s32[8]{0:T(128)}, s32[8]{0:T(128)S(1)}, u32[]{:S(2)}) copy-start(s32[8]{0:T(128)S(1)} %get-tuple-element.111) | copy-start | bytes 100
  16.1 13.1 %copy-start.9 = (s32[6,1]{1,0:T(8,128)}, s32[6,1]{1,0:T(8,128)S(1)}, u32[]{:S(2)}) copy-start(s32[6,1]{1,0:T(8,128)S(1)} %constant_dynamic-slice_fusion.10) | copy-start | bytes 76
  16.2 13.0 %copy-start.15 = (s32[33,8]{0,1:T(8,128)}, s32[33,8]{0,1:T(8,128)S(1)}, u32[]{:S(2)}) copy-start(s32[33,8]{0,1:T(8,128)S(1)} %convert_reduce_fusion.3) | copy-start | bytes 3172
  29.2 24.2 %collective-permute-start.7 = (bf16[48,4,16,128]{3,2,1,0:T(8,128)(2,1)}, bf16[48,4,16,128]{3,2,1,0:T(8,128)(2,1)}, u32[]{:S(2)}, u32[]{:S(2)}) collective-permute-start(bf16[48,4,16,128]{3,2,1,0:T(8,128)(2,1)} %compact.6.refs_0_), channel_id=1, source_target_pairs={{0,8},{8,0},{16,24},{24,16},{1,9},{9,1},{17,25},{25,17},{2,10},{10... | collective-permute-start | bytes 2359304 | tf_op jit(solution)/shard_map/ppermute | solution.py:672
  30.8 22.6 %collective-permute-start.6 = (bf16[48,4,16,128]{3,2,1,0:T(8,128)(2,1)}, bf16[48,4,16,128]{3,2,1,0:T(8,128)(2,1)}, u32[]{:S(2)}, u32[]{:S(2)}) collective-permute-start(bf16[48,4,16,128]{3,2,1,0:T(8,128)(2,1)} %compact.6.refs_0_), channel_id=1, source_target_pairs={{0,16},{8,24},{16,0},{24,8},{1,17},{9,25},{17,1},{25,9},{2,18},{10... | collective-permute-start | bytes 2359304 | tf_op jit(solution)/shard_map/ppermute | solution.py:672
  54.0 11.9 %collective-permute-start.11 = (bf16[104,4,16,128]{3,2,1,0:T(8,128)(2,1)}, bf16[104,4,16,128]{3,2,1,0:T(8,128)(2,1)S(1)}, u32[]{:S(2)}, u32[]{:S(2)}) collective-permute-start(bf16[104,4,16,128]{3,2,1,0:T(8,128)(2,1)} %after.15.refs_4_), channel_id=1, source_target_pairs={{0,8},{8,0},{16,24},{24,16},{1,9},{9,1},{17,25},{25,17},{2,10},{10... | collective-permute-start | bytes 5111816 | tf_op jit(solution)/shard_map/ppermute | solution.py:672
  54.4 53.6 %collective-permute-start.13 = (bf16[104,4,16,128]{3,2,1,0:T(8,128)(2,1)}, bf16[104,4,16,128]{3,2,1,0:T(8,128)(2,1)}, u32[]{:S(2)}, u32[]{:S(2)}) collective-permute-start(bf16[104,4,16,128]{3,2,1,0:T(8,128)(2,1)} %after.15.refs_4_), channel_id=1, source_target_pairs={{0,16},{8,24},{16,0},{24,8},{1,17},{9,25},{17,1},{25,9},{2,18},{10... | collective-permute-start | bytes 5111816 | tf_op jit(solution)/shard_map/ppermute | solution.py:672
  57.3 50.6 %collective-permute-start.8 = (bf16[4,384,512]{2,1,0:T(8,128)(2,1)}, bf16[4,384,512]{2,1,0:T(8,128)(2,1)}, u32[]{:S(2)}, u32[]{:S(2)}) collective-permute-start(bf16[4,384,512]{2,1,0:T(8,128)(2,1)} %after.12), channel_id=1, source_target_pairs={{0,1},{1,0},{2,3},{3,2},{4,5},{5,4},{6,7},{7,6},{8,9},{9,8},{10,11... | collective-permute-start | bytes 4718600 | tf_op jit(solution)/shard_map/ppermute | solution.py:585
  58.1 49.8 %collective-permute-start.9 = (bf16[4,384,512]{2,1,0:T(8,128)(2,1)}, bf16[4,384,512]{2,1,0:T(8,128)(2,1)}, u32[]{:S(2)}, u32[]{:S(2)}) collective-permute-start(bf16[4,384,512]{2,1,0:T(8,128)(2,1)} %after.13.refs_1_), channel_id=1, source_target_pairs={{2,4},{3,5},{4,6},{5,7},{10,12},{11,13},{12,14},{13,15},{18,20},{1... | collective-permute-start | bytes 4718600 | tf_op jit(solution)/shard_map/ppermute | solution.py:591
  60.1 9.0 %copy-start.8 = (s32[8,8]{1,0:T(8,128)S(1)}, s32[8,8]{1,0:T(8,128)}, u32[]{:S(2)}) copy-start(s32[8,8]{1,0:T(8,128)} %copy-done.7) | copy-start | bytes 772
  60.1 9.6 %copy-start.12 = (s32[8,8]{1,0:T(8,128)S(1)}, s32[8,8]{1,0:T(8,128)}, u32[]{:S(2)}) copy-start(s32[8,8]{1,0:T(8,128)} %copy-done.11) | copy-start | bytes 772
  60.1 10.2 %copy-start.17 = (s32[8,8]{1,0:T(8,128)S(1)}, s32[8,8]{1,0:T(8,128)}, u32[]{:S(2)}) copy-start(s32[8,8]{1,0:T(8,128)} %get-tuple-element.124) | copy-start | bytes 772
  60.1 12.2 %copy-start.5 = (s32[24,128]{1,0:T(8,128)S(1)}, s32[24,128]{1,0:T(8,128)}, u32[]{:S(2)}) copy-start(s32[24,128]{1,0:T(8,128)} %copy-done.4) | copy-start | bytes 36868
  60.1 12.2 %copy-start.6 = (s32[8,384]{1,0:T(8,128)S(1)}, s32[8,384]{1,0:T(8,128)}, u32[]{:S(2)}) copy-start(s32[8,384]{1,0:T(8,128)} %get-tuple-element.94) | copy-start | bytes 36868
  60.1 47.9 %collective-permute-start.10 = (bf16[4,384,512]{2,1,0:T(8,128)(2,1)}, bf16[4,384,512]{2,1,0:T(8,128)(2,1)}, u32[]{:S(2)}, u32[]{:S(2)}) collective-permute-start(bf16[4,384,512]{2,1,0:T(8,128)(2,1)} %after.14.refs_4_), channel_id=1, source_target_pairs={{2,0},{3,1},{4,2},{5,3},{10,8},{11,9},{12,10},{13,11},{18,16},{19,... | collective-permute-start | bytes 4718600 | tf_op jit(solution)/shard_map/ppermute | solution.py:592
  65.9 1.3 copy-start.2
  67.8 40.2 %collective-permute-start.12 = (bf16[48,4,16,128]{3,2,1,0:T(8,128)(2,1)}, bf16[48,4,16,128]{3,2,1,0:T(8,128)(2,1)}, u32[]{:S(2)}, u32[]{:S(2)}) collective-permute-start(bf16[48,4,16,128]{3,2,1,0:T(8,128)(2,1)} %after.16.refs_2_), channel_id=1, source_target_pairs={{0,8},{8,0},{16,24},{24,16},{1,9},{9,1},{17,25},{25,17},{2,10},{10... | collective-permute-start | bytes 2359304 | tf_op jit(solution)/shard_map/ppermute | solution.py:684
  108.6 8.2 %collective-permute-start.16 = (bf16[104,4,16,128]{3,2,1,0:T(8,128)(2,1)}, bf16[104,4,16,128]{3,2,1,0:T(8,128)(2,1)S(1)}, u32[]{:S(2)}, u32[]{:S(2)}) collective-permute-start(bf16[104,4,16,128]{3,2,1,0:T(8,128)(2,1)} %after.17.refs_8_), channel_id=1, source_target_pairs={{0,8},{8,0},{16,24},{24,16},{1,9},{9,1},{17,25},{25,17},{2,10},{10... | collective-permute-start | bytes 5111816 | tf_op jit(solution)/shard_map/ppermute | solution.py:672
  111.4 35.2 %collective-permute-start.20 = (bf16[4,384,512]{2,1,0:T(8,128)(2,1)}, bf16[4,384,512]{2,1,0:T(8,128)(2,1)}, u32[]{:S(2)}, u32[]{:S(2)}) collective-permute-start(bf16[4,384,512]{2,1,0:T(8,128)(2,1)} %after.19.refs_2_), channel_id=1, source_target_pairs={{4,6},{5,7},{12,14},{13,15},{20,22},{21,23},{28,30},{29,31}} | collective-permute-start | bytes 4718600 | tf_op jit(solution)/shard_map/ppermute | solution.py:591
  113.8 38.6 %collective-permute-start.18 = (bf16[104,4,16,128]{3,2,1,0:T(8,128)(2,1)}, bf16[104,4,16,128]{3,2,1,0:T(8,128)(2,1)}, u32[]{:S(2)}, u32[]{:S(2)}) collective-permute-start(bf16[104,4,16,128]{3,2,1,0:T(8,128)(2,1)} %after.17.refs_8_), channel_id=1, source_target_pairs={{0,16},{8,24},{16,0},{24,8},{1,17},{9,25},{17,1},{25,9},{2,18},{10... | collective-permute-start | bytes 5111816 | tf_op jit(solution)/shard_map/ppermute | solution.py:672
  115.0 39.7 %collective-permute-start.21 = (bf16[4,384,512]{2,1,0:T(8,128)(2,1)}, bf16[4,384,512]{2,1,0:T(8,128)(2,1)}, u32[]{:S(2)}, u32[]{:S(2)}) collective-permute-start(bf16[4,384,512]{2,1,0:T(8,128)(2,1)} %after.20.refs_5_), channel_id=1, source_target_pairs={{2,0},{3,1},{10,8},{11,9},{18,16},{19,17},{26,24},{27,25}} | collective-permute-start | bytes 4718600 | tf_op jit(solution)/shard_map/ppermute | solution.py:592
  116.9 1.3 copy-start.1
  118.8 39.3 %collective-permute-start.17 = (bf16[104,4,16,128]{3,2,1,0:T(8,128)(2,1)}, bf16[104,4,16,128]{3,2,1,0:T(8,128)(2,1)}, u32[]{:S(2)}, u32[]{:S(2)}) collective-permute-start(bf16[104,4,16,128]{3,2,1,0:T(8,128)(2,1)} %after.18.refs_6_), channel_id=1, source_target_pairs={{0,8},{8,0},{16,24},{24,16},{1,9},{9,1},{17,25},{25,17},{2,10},{10... | collective-permute-start | bytes 5111816 | tf_op jit(solution)/shard_map/ppermute | solution.py:684
  119.5 38.5 %collective-permute-start.22 = (bf16[4,384,512]{2,1,0:T(8,128)(2,1)}, bf16[4,384,512]{2,1,0:T(8,128)(2,1)}, u32[]{:S(2)}, u32[]{:S(2)}) collective-permute-start(bf16[4,384,512]{2,1,0:T(8,128)(2,1)} %after.21), channel_id=1, source_target_pairs={{0,1},{1,0},{2,3},{3,2},{4,5},{5,4},{6,7},{7,6},{8,9},{9,8},{10,11... | collective-permute-start | bytes 4718600 | tf_op jit(solution)/shard_map/ppermute | solution.py:585
  146.5 80.5 %collective-permute-start.15 = (bf16[192,4,16,128]{3,2,1,0:T(8,128)(2,1)}, bf16[192,4,16,128]{3,2,1,0:T(8,128)(2,1)S(1)}, u32[]{:S(2)}, u32[]{:S(2)}) collective-permute-start(bf16[192,4,16,128]{3,2,1,0:T(8,128)(2,1)} %compact.9.refs_6_.refs_0_), channel_id=1, source_target_pairs={{0,16},{8,24},{16,0},{24,8},{1,17},{9,25},{17,1},{25,9},{2,18},{10... | collective-permute-start | bytes 9437192 | tf_op jit(solution)/shard_map/ppermute | solution.py:672
  152.4 49.8 %collective-permute-start.19 = (bf16[104,4,16,128]{3,2,1,0:T(8,128)(2,1)}, bf16[104,4,16,128]{3,2,1,0:T(8,128)(2,1)}, u32[]{:S(2)}, u32[]{:S(2)}) collective-permute-start(bf16[104,4,16,128]{3,2,1,0:T(8,128)(2,1)} %collective-permute-done.18.refs_4_.refs_10_), channel_id=1, source_target_pairs={{0,8},{8,0},{16,24},{24,16},{1,9},{9,1},{17,25},{25,17},{2,10},{10... | collective-permute-start | bytes 5111816 | tf_op jit(solution)/shard_map/ppermute | solution.py:700
  158.6 0.7 copy-start.19
  158.6 36.3 %collective-permute-start.23 = (bf16[4,384,512]{2,1,0:T(8,128)(2,1)}, bf16[4,384,512]{2,1,0:T(8,128)(2,1)}, u32[]{:S(2)}, u32[]{:S(2)}) collective-permute-start(bf16[4,384,512]{2,1,0:T(8,128)(2,1)} %after.22), channel_id=1, source_target_pairs={{0,1},{1,0},{2,3},{3,2},{4,5},{5,4},{6,7},{7,6},{8,9},{9,8},{10,11... | collective-permute-start | bytes 4718600 | tf_op jit(solution)/shard_map/ppermute | solution.py:585
  162.6 70.1 %collective-permute-start.14 = (bf16[192,4,16,128]{3,2,1,0:T(8,128)(2,1)}, bf16[192,4,16,128]{3,2,1,0:T(8,128)(2,1)}, u32[]{:S(2)}, u32[]{:S(2)}) collective-permute-start(bf16[192,4,16,128]{3,2,1,0:T(8,128)(2,1)} %compact.9.refs_6_.refs_0_), channel_id=1, source_target_pairs={{0,8},{8,0},{16,24},{24,16},{1,9},{9,1},{17,25},{25,17},{2,10},{10... | collective-permute-start | bytes 9437192 | tf_op jit(solution)/shard_map/ppermute | solution.py:672
  227.0 2.5 copy-start.10
  227.0 3.0 %copy-start.14 = (s32[8]{0:T(128)S(1)}, s32[8]{0:T(128)}, u32[]{:S(2)}) copy-start(s32[8]{0:T(128)} %copy-done.13) | copy-start | bytes 100
  227.0 3.0 %copy-start.21 = (s32[8]{0:T(128)S(1)}, s32[8]{0:T(128)}, u32[]{:S(2)}) copy-start(s32[8]{0:T(128)} %copy-done.20) | copy-start | bytes 100
  227.0 5.0 %copy-start.16 = (s32[528]{0:T(1024)S(1)}, s32[528]{0:T(1024)}, u32[]{:S(2)}) copy-start(s32[528]{0:T(1024)} %get-tuple-element.127) | copy-start | bytes 6340
  227.0 1.6 copy-start.3
  228.7 6.4 %collective-permute-start.24 = (bf16[192,4,16,128]{3,2,1,0:T(8,128)(2,1)}, bf16[192,4,16,128]{3,2,1,0:T(8,128)(2,1)}, u32[]{:S(2)}, u32[]{:S(2)}) collective-permute-start(bf16[192,4,16,128]{3,2,1,0:T(8,128)(2,1)} %after.23.refs_2_), channel_id=1, source_target_pairs={{0,8},{8,0},{16,24},{24,16},{1,9},{9,1},{17,25},{25,17},{2,10},{10... | collective-permute-start | bytes 9437192 | tf_op jit(solution)/shard_map/ppermute | solution.py:716

commit v2 on v1

--- a/solution.py
+++ b/solution.py
@@ -16,7 +16,7 @@
 STRIDE = 1024
 VMEM = 56 * 2**20
 COST = pl.CostEstimate(flops=10**6, bytes_accessed=10**6, transcendentals=0)
-CHUNKS = ((48, 5), (104, 10), (104, 10), (192, 20))
+CHUNKS = ((40, 4), (104, 10), (112, 11), (192, 20))
 
 
 def before(values):

time: 262 us -> 264 us (level); the launches traced: 262 us -> 260 us
  Pallas kernels: 170 us -> 166 us
    pallas_call x4, Pallas kernels: 74.7 us -> 71.1 us  [compact(): pl.pallas_call(compact_kernel, grid_spec=pltpu.PrefetchScalarGridSpec(num...]
    ppermute x8, waiting for transfers between devices: 4.66 us -> 7.55 us  [exchange(): return (lax.ppermute(units, 'occ', chip), lax.ppermute(units, 'occ', core))]
  transfers between devices with their start and end apart: 22 -> 22, of which waited for: 4 -> 4; matrix products, arithmetic and copies ran while one was open for 14% -> 15% of each run, Pallas kernels for 54% -> 53%
where the time goes in v2:
time: 264 us; the launch traced here: 260 us
  Pallas kernels  166 us (63%)
  starting transfers between devices  34.9 us (13%)
  local copies, waits for them, and re-layouts  23.3 us (9%)
  other arithmetic  18.1 us (7%)
  waiting for transfers between devices  15.2 us (6%)
    pallas_call x4, Pallas kernels, compact(): pl.pallas_call(compact_kernel, grid_spec=pltpu.PrefetchScalarGridSpec(num...  71.1 us
    pallas_call x2, Pallas kernels, multiply(): pl.pallas_call(functools.partial(multiply_kernel, low, high), grid_spec=p...  41.2 us
    pallas_call x3, Pallas kernels, add_shards(): pl.pallas_call(functools.partial(add_kernel, len(buffers), low), grid_spe...  40 us
    pallas_call x1, Pallas kernels, restore(): pl.pallas_call(restore_kernel, grid_spec=pltpu.PrefetchScalarGridSpec(num...  10 us
    ppermute x3, starting transfers between devices, step(): lax.ppermute(down, 'vir', [(i, i - 2) for i in range(2, count - 2 * k)])  9.62 us
    ppermute x3, starting transfers between devices, step(): lax.ppermute(up, 'vir', [(i, i + 2) for i in range(2 * k, count - 2)])  8.85 us
    select_n x3, other arithmetic, pick(): chosen = jnp.where(line >= at, kinds[at], chosen)  8.76 us
    broadcast_in_dim x1, local copies, waits for them, and re-layouts, on_device(): jnp.zeros((LABELS, amplitudes.shape[0], pieces, PIECE, amplitudes.shape[2...  8.49 us
  transfers between devices with their start and end apart: 22, of which 4 were waited for; matrix products, arithmetic and copies ran while one was open for 15% of the time, Pallas kernels for 53%

profile of v2, /device:TPU:17, one launch (start us, length us, event | category | flops | bytes accessed | tf_op | source)
XLA Modules:
  0.0 260.0 jit_solution(9207200093896613467)
XLA Ops:
  0.0 1.2 collective-permute-start.5
  1.2 2.1 collective-permute-start.4
  3.3 4.3 %collective-permute-start.3 = (bf16[4,384,512]{2,1,0:T(8,128)(2,1)}, bf16[4,384,512]{2,1,0:T(8,128)(2,1)}, u32[]{:S(2)}, u32[]{:S(2)}) collective-permute-start(bf16[4,384,512]{2,1,0:T(8,128)(2,1)} %refs_0_.13), channel_id=1, source_target_pairs={{0,2},{1,3},{2,4},{3,5},{4,6},{5,7},{8,10},{9,11},{10,12},{11,13},... | collective-permute-start | bytes 4718600 | tf_op jit(solution)/shard_map/ppermute | solution.py:591
  7.7 0.7 eq.198
  8.4 0.8 dynamic_slice.48
  9.2 1.1 convert_reduce_fusion
  10.9 0.9 fusion.2
  12.3 0.6 add_select_fusion
  12.9 0.7 select_reduce_fusion.1
  14.1 0.7 select_reduce_fusion.5
  16.3 0.7 slice_reduce_fusion
  17.3 0.6 broadcast_maximum_fusion
  17.9 0.7 multiply_add_fusion
  18.7 6.9 %compact.6.refs_0_ = bf16[40,4,16,128]{3,2,1,0:T(8,128)(2,1)} custom-call(s32[2]{0:T(128)} %get-tuple-element.108.span, s32[33]{0:T(128)S(1)} %get-tuple-element.132.label, s32[33]{0:T(128)S(1)} %fusion.34.unit, s32[33]{0:T(128)S(1)} %get-tuple-element.133.tiles, s32[33]{0:T(128)S(1)} %fusion.36.depth, s32[528]{0:T(1024)S(1)} %get-tuple-element.126.orbital, ...), custom_call_target="tpu_custom_call" | custom-call | flops 1000000 | bytes 1000000 | tf_op jit(solution)/shard_map/compact/pallas_call | solution.py:261
  25.7 1.6 collective-permute-start.7
  27.2 1.2 collective-permute-start.6
  28.5 19.8 %compact.7.refs_5_.refs_0_ = bf16[104,4,16,128]{3,2,1,0:T(8,128)(2,1)} custom-call(s32[2]{0:T(128)} %get-tuple-element.107.span, s32[33]{0:T(128)S(1)} %get-tuple-element.132.label, s32[33]{0:T(128)S(1)} %fusion.34.unit, s32[33]{0:T(128)S(1)} %get-tuple-element.133.tiles, s32[33]{0:T(128)S(1)} %fusion.36.depth, s32[528]{0:T(1024)S(1)} %get-tuple-element.126.orbital, ...), custom_call_target="tpu_custom_call" | custom-call | flops 1000000 | bytes 1000000 | tf_op jit(solution)/shard_map/compact/pallas_call | solution.py:261
  48.3 0.6 token_.7.refs_1_.refs_16_.refs_12_
  49.5 2.7 %broadcast_select_fusion.refs_0_ = bf16[4,384,512]{2,1,0:T(8,128)(2,1)} fusion(bf16[4,384,512]{2,1,0:T(8,128)(2,1)} %collective-permute-done.3.refs_1_.refs_0_, bf16[4,384,512]{2,1,0:T(8,128)(2,1)} %collective-permute-done.4.refs_2_.refs_0_, pred[]{:T(512)S(6)} %ge.50), kind=kLoop, calls=%fused_computation.3 | loop fusion | flops 786432 | bytes 4718593 | tf_op jit(solution)/shard_map/jit(_where)/select_n | solution.py:601
  52.6 2.0 collective-permute-start.9
  54.7 5.8 %collective-permute-start.10 = (bf16[4,384,512]{2,1,0:T(8,128)(2,1)}, bf16[4,384,512]{2,1,0:T(8,128)(2,1)}, u32[]{:S(2)}, u32[]{:S(2)}) collective-permute-start(bf16[4,384,512]{2,1,0:T(8,128)(2,1)} %after.14.refs_4_), channel_id=1, source_target_pairs={{2,0},{3,1},{4,2},{5,3},{10,8},{11,9},{12,10},{13,11},{18,16},{19,... | collective-permute-start | bytes 4718600 | tf_op jit(solution)/shard_map/ppermute | solution.py:592
  60.5 0.6 reshape.404.pieces
  61.1 0.7 reshape.405.piece_from
  61.7 0.6 reshape.406.piece_to
  62.4 1.2 copy-done.2
  63.6 0.6 token_.8.refs_1_
  64.2 1.3 collective-permute-start.12
  66.2 0.6 select_reduce_fusion.16.order
  66.8 0.6 reshape_add_fusion.slot_ref
  67.4 19.3 %compact.8.refs_13_.refs_7_.refs_0_ = bf16[112,4,16,128]{3,2,1,0:T(8,128)(2,1)} custom-call(s32[2]{0:T(128)} %get-tuple-element.106.span, s32[33]{0:T(128)S(1)} %get-tuple-element.132.label, s32[33]{0:T(128)S(1)} %fusion.34.unit, s32[33]{0:T(128)S(1)} %get-tuple-element.133.tiles, s32[33]{0:T(128)S(1)} %fusion.36.depth, s32[528]{0:T(1024)S(1)} %get-tuple-element.126.orbital, ...), custom_call_target="tpu_custom_call" | custom-call | flops 1000000 | bytes 1000000 | tf_op jit(solution)/shard_map/compact/pallas_call | solution.py:261
  87.3 8.5 %broadcast_in_dim.300.refs_11_ = bf16[8,4,48,16,512]{4,3,2,1,0:T(8,128)(2,1)} broadcast(bf16[]{:T(256)} %constant.226.clone.1), dimensions={} | broadcast | bytes 25165826 | tf_op jit(solution)/shard_map/broadcast_in_dim | solution.py:659
  95.8 6.9 %add_shards.3.refs_4_.refs_11_ = bf16[8,4,48,16,512]{4,3,2,1,0:T(8,128)(2,1)} custom-call(s32[8]{0:T(128)} %select_reduce_fusion.16.order, s32[8]{0:T(128)} %compare_select_fusion.5.source, s32[8]{0:T(128)} %broadcast.786.row, s32[64]{0:T(128)} %reshape.404.pieces, s32[64]{0:T(128)} %reshape.405.piece_from, ...), custom_call_target="tpu_custom_call", output_to_operand_aliasing={{}: (18, {})} | custom-call | flops 1000000 | bytes 1000000 | tf_op jit(solution)/shard_map/add_shards/pallas_call | solution.py:361
  102.8 0.6 token_.9.refs_16_.refs_1_
  103.4 2.7 %select_select_fusion.1.refs_0_ = bf16[4,384,512]{2,1,0:T(8,128)(2,1)} fusion(bf16[4,384,512]{2,1,0:T(8,128)(2,1)} %collective-permute-done.9.refs_1_.refs_0_, bf16[4,384,512]{2,1,0:T(8,128)(2,1)} %after.14.refs_4_, bf16[4,384,512]{2,1,0:T(8,128)(2,1)} %collective-permute-done.10.refs_2_.refs_0_, pred[]{:T(512)S(6)} %ge.51, pred[]{:T(512)S(6)} %ge.50), kind=kLoop, calls=%fused_computation.2 | loop fusion | flops 1572864 | bytes 6291458 | tf_op jit(solution)/shard_map/jit(_where)/select_n | solution.py:601
  106.1 2.5 collective-permute-start.20
  108.6 1.2 collective-permute-start.18
  109.8 1.8 collective-permute-start.21
  111.6 1.2 copy-done.1
  112.8 0.6 token_.10.refs_1_
  113.4 0.8 collective-permute-start.17
  114.2 1.9 collective-permute-start.22
  116.0 25.1 %compact.9.refs_6_.refs_0_ = bf16[192,4,16,128]{3,2,1,0:T(8,128)(2,1)} custom-call(s32[2]{0:T(128)} %get-tuple-element.109.span, s32[33]{0:T(128)S(1)} %get-tuple-element.132.label, s32[33]{0:T(128)S(1)} %fusion.34.unit, s32[33]{0:T(128)S(1)} %get-tuple-element.133.tiles, s32[33]{0:T(128)S(1)} %fusion.36.depth, s32[528]{0:T(1024)S(1)} %get-tuple-element.126.orbital, ...), custom_call_target="tpu_custom_call" | custom-call | flops 1000000 | bytes 1000000 | tf_op jit(solution)/shard_map/compact/pallas_call | solution.py:261
  141.3 1.2 collective-permute-start.15
  142.5 7.5 %collective-permute-done.18.refs_4_.refs_10_ = bf16[112,4,16,128]{3,2,1,0:T(8,128)(2,1)} collective-permute-done((bf16[112,4,16,128]{3,2,1,0:T(8,128)(2,1)}, bf16[112,4,16,128]{3,2,1,0:T(8,128)(2,1)}, u32[]{:S(2)}, u32[]{:S(2)}) %collective-permute-start.18) | collective-permute-done | bytes 1835040 | tf_op jit(solution)/shard_map/ppermute | solution.py:672
  150.0 2.3 collective-permute-start.19
  152.3 3.3 %select_select_fusion.refs_0_ = bf16[4,384,512]{2,1,0:T(8,128)(2,1)} fusion(bf16[4,384,512]{2,1,0:T(8,128)(2,1)} %collective-permute-done.20.refs_1_.refs_3_, bf16[4,384,512]{2,1,0:T(8,128)(2,1)} %after.19.refs_2_, bf16[4,384,512]{2,1,0:T(8,128)(2,1)} %after.20.refs_5_, bf16[4,384,512]{2,1,0:T(8,128)(2,1)} %collective-permute-done.21.refs_2_.refs_6_, ...), kind=kLoop, calls=%fused_computation.1 | loop fusion | flops 2359296 | bytes 7864323 | tf_op jit(solution)/shard_map/jit(_where)/select_n | solution.py:601
  155.6 0.6 token_.11.refs_1_
  156.2 1.9 collective-permute-start.23
  158.1 0.7 fusion.28.span
  158.8 1.3 fusion.39.chunk
  160.1 1.3 fusion.37
  161.6 26.0 %add_shards.4.refs_11_.refs_0_ = bf16[8,4,48,16,512]{4,3,2,1,0:T(8,128)(2,1)} custom-call(s32[8]{0:T(128)} %select_reduce_fusion.16.order, s32[8]{0:T(128)} %compare_select_fusion.5.source, s32[8]{0:T(128)} %broadcast.786.row, s32[64]{0:T(128)} %reshape.404.pieces, s32[64]{0:T(128)} %reshape.405.piece_from, ...), custom_call_target="tpu_custom_call", output_to_operand_aliasing={{}: (18, {})} | custom-call | flops 1000000 | bytes 1000000 | tf_op jit(solution)/shard_map/add_shards/pallas_call | solution.py:361
  187.6 0.6 token_.13.refs_0_
  188.2 4.9 %collective-permute-done.23.refs_10_ = bf16[4,384,512]{2,1,0:T(8,128)(2,1)} collective-permute-done((bf16[4,384,512]{2,1,0:T(8,128)(2,1)}, bf16[4,384,512]{2,1,0:T(8,128)(2,1)}, u32[]{:S(2)}, u32[]{:S(2)}) %collective-permute-start.23) | collective-permute-done | bytes 1572896 | tf_op jit(solution)/shard_map/ppermute | solution.py:585
  193.2 7.2 %add_shards.5.refs_12_.refs_8_ = bf16[8,4,48,16,512]{4,3,2,1,0:T(8,128)(2,1)} custom-call(s32[8]{0:T(128)} %select_reduce_fusion.16.order, s32[8]{0:T(128)} %compare_select_fusion.5.source, s32[8]{0:T(128)} %broadcast.786.row, s32[64]{0:T(128)} %reshape.404.pieces, s32[64]{0:T(128)} %reshape.405.piece_from, ...), custom_call_target="tpu_custom_call", output_to_operand_aliasing={{}: (18, {})} | custom-call | flops 1000000 | bytes 1000000 | tf_op jit(solution)/shard_map/add_shards/pallas_call | solution.py:361
  200.3 23.8 %multiply.4.refs_0_.refs_9_ = bf16[16,33,16,512]{3,2,1,0:T(8,128)(2,1)} custom-call(s32[2]{0:T(128)} %fusion.28.span, s32[33]{0:T(128)S(1)} %get-tuple-element.132.label, s32[33]{0:T(128)S(1)} %fusion.34.unit, s32[33]{0:T(128)S(1)} %get-tuple-element.133.tiles, s32[33]{0:T(128)S(1)} %fusion.36.depth, s32[33]{0:T(128)} %get-tuple-element.134.label_end, ...), custom_call_target="tpu_custom_call" | custom-call | flops 1000000 | bytes 1000000 | tf_op jit(solution)/shard_map/multiply/pallas_call | solution.py:494
  224.1 0.6 token_.12.refs_1_
  224.8 1.6 copy-done.3
  227.5 0.6 subtract_reduce_fusion.1
  228.8 0.8 fusion.27.span
  229.6 0.6 sub.114.orbital_ref
  230.2 2.4 collective-permute-done.24.refs_3_
  232.6 17.4 %multiply.5.in_ref = bf16[16,33,16,512]{3,2,1,0:T(8,128)(2,1)} custom-call(s32[2]{0:T(128)} %fusion.27.span, s32[33]{0:T(128)S(1)} %get-tuple-element.132.label, s32[33]{0:T(128)S(1)} %fusion.34.unit, s32[33]{0:T(128)S(1)} %get-tuple-element.133.tiles, s32[33]{0:T(128)S(1)} %fusion.36.depth, ...), custom_call_target="tpu_custom_call", output_to_operand_aliasing={{}: (18, {})} | custom-call | flops 1000000 | bytes 1000000 | tf_op jit(solution)/shard_map/multiply/pallas_call | solution.py:494
  250.0 10.0 %restore.1 = bf16[16,384,512]{2,1,0:T(8,128)(2,1)} custom-call(s32[1]{0:T(128)} %bitcast.7.live, s32[1,528]{1,0:T(1,128)} %sub.114.orbital_ref, bf16[16,33,16,512]{3,2,1,0:T(8,128)(2,1)} %multiply.5.in_ref), custom_call_target="tpu_custom_call" | custom-call | flops 1000000 | bytes 1000000 | tf_op jit(solution)/shard_map/restore/pallas_call | solution.py:541
  (133 shorter events, 7.3 us)
Async XLA Ops:
  0.0 48.3 %collective-permute-start.5 = (bf16[4,384,512]{2,1,0:T(8,128)(2,1)}, bf16[4,384,512]{2,1,0:T(8,128)(2,1)}, u32[]{:S(2)}, u32[]{:S(2)}) collective-permute-start(bf16[4,384,512]{2,1,0:T(8,128)(2,1)} %refs_0_.13), channel_id=1, source_target_pairs={{0,1},{1,0},{2,3},{3,2},{4,5},{5,4},{6,7},{7,6},{8,9},{9,8},{10,11... | collective-permute-start | bytes 4718600 | tf_op jit(solution)/shard_map/ppermute | solution.py:585
  1.2 47.0 %collective-permute-start.4 = (bf16[4,384,512]{2,1,0:T(8,128)(2,1)}, bf16[4,384,512]{2,1,0:T(8,128)(2,1)}, u32[]{:S(2)}, u32[]{:S(2)}) collective-permute-start(bf16[4,384,512]{2,1,0:T(8,128)(2,1)} %refs_0_.13), channel_id=1, source_target_pairs={{2,0},{3,1},{4,2},{5,3},{6,4},{7,5},{10,8},{11,9},{12,10},{13,11},... | collective-permute-start | bytes 4718600 | tf_op jit(solution)/shard_map/ppermute | solution.py:592
  3.3 45.0 %collective-permute-start.3 = (bf16[4,384,512]{2,1,0:T(8,128)(2,1)}, bf16[4,384,512]{2,1,0:T(8,128)(2,1)}, u32[]{:S(2)}, u32[]{:S(2)}) collective-permute-start(bf16[4,384,512]{2,1,0:T(8,128)(2,1)} %refs_0_.13), channel_id=1, source_target_pairs={{0,2},{1,3},{2,4},{3,5},{4,6},{5,7},{8,10},{9,11},{10,12},{11,13},... | collective-permute-start | bytes 4718600 | tf_op jit(solution)/shard_map/ppermute | solution.py:591
  11.9 13.7 %copy-start.4 = (s32[24,128]{1,0:T(8,128)}, s32[24,128]{1,0:T(8,128)S(1)}, u32[]{:S(2)}) copy-start(s32[24,128]{1,0:T(8,128)S(1)} %fusion.2) | copy-start | bytes 36868
  12.2 13.4 %copy-start.7 = (s32[8,8]{1,0:T(8,128)}, s32[8,8]{1,0:T(8,128)S(1)}, u32[]{:S(2)}) copy-start(s32[8,8]{1,0:T(8,128)S(1)} %fusion.12) | copy-start | bytes 772
  12.3 13.4 %copy-start.11 = (s32[8,8]{1,0:T(8,128)}, s32[8,8]{1,0:T(8,128)S(1)}, u32[]{:S(2)}) copy-start(s32[8,8]{1,0:T(8,128)S(1)} %select_reduce_fusion.3) | copy-start | bytes 772
  13.7 11.9 %copy-start.13 = (s32[8]{0:T(128)}, s32[8]{0:T(128)S(1)}, u32[]{:S(2)}) copy-start(s32[8]{0:T(128)S(1)} %get-tuple-element.130) | copy-start | bytes 100
  15.5 0.6 copy-start.18
  15.7 10.0 %copy-start.20 = (s32[8]{0:T(128)}, s32[8]{0:T(128)S(1)}, u32[]{:S(2)}) copy-start(s32[8]{0:T(128)S(1)} %get-tuple-element.111) | copy-start | bytes 100
  16.1 9.5 %copy-start.9 = (s32[6,1]{1,0:T(8,128)}, s32[6,1]{1,0:T(8,128)S(1)}, u32[]{:S(2)}) copy-start(s32[6,1]{1,0:T(8,128)S(1)} %constant_dynamic-slice_fusion.10) | copy-start | bytes 76
  16.2 9.5 %copy-start.15 = (s32[33,8]{0,1:T(8,128)}, s32[33,8]{0,1:T(8,128)S(1)}, u32[]{:S(2)}) copy-start(s32[33,8]{0,1:T(8,128)S(1)} %convert_reduce_fusion.3) | copy-start | bytes 3172
  25.7 22.6 %collective-permute-start.7 = (bf16[40,4,16,128]{3,2,1,0:T(8,128)(2,1)}, bf16[40,4,16,128]{3,2,1,0:T(8,128)(2,1)}, u32[]{:S(2)}, u32[]{:S(2)}) collective-permute-start(bf16[40,4,16,128]{3,2,1,0:T(8,128)(2,1)} %compact.6.refs_0_), channel_id=1, source_target_pairs={{0,8},{8,0},{16,24},{24,16},{1,9},{9,1},{17,25},{25,17},{2,10},{10... | collective-permute-start | bytes 1966088 | tf_op jit(solution)/shard_map/ppermute | solution.py:672
  27.2 21.0 %collective-permute-start.6 = (bf16[40,4,16,128]{3,2,1,0:T(8,128)(2,1)}, bf16[40,4,16,128]{3,2,1,0:T(8,128)(2,1)}, u32[]{:S(2)}, u32[]{:S(2)}) collective-permute-start(bf16[40,4,16,128]{3,2,1,0:T(8,128)(2,1)} %compact.6.refs_0_), channel_id=1, source_target_pairs={{0,16},{8,24},{16,0},{24,8},{1,17},{9,25},{17,1},{25,9},{2,18},{10... | collective-permute-start | bytes 1966088 | tf_op jit(solution)/shard_map/ppermute | solution.py:672
  48.9 13.5 %collective-permute-start.11 = (bf16[104,4,16,128]{3,2,1,0:T(8,128)(2,1)}, bf16[104,4,16,128]{3,2,1,0:T(8,128)(2,1)S(1)}, u32[]{:S(2)}, u32[]{:S(2)}) collective-permute-start(bf16[104,4,16,128]{3,2,1,0:T(8,128)(2,1)} %after.15.refs_4_), channel_id=1, source_target_pairs={{0,8},{8,0},{16,24},{24,16},{1,9},{9,1},{17,25},{25,17},{2,10},{10... | collective-permute-start | bytes 5111816 | tf_op jit(solution)/shard_map/ppermute | solution.py:672
  49.2 53.5 %collective-permute-start.13 = (bf16[104,4,16,128]{3,2,1,0:T(8,128)(2,1)}, bf16[104,4,16,128]{3,2,1,0:T(8,128)(2,1)}, u32[]{:S(2)}, u32[]{:S(2)}) collective-permute-start(bf16[104,4,16,128]{3,2,1,0:T(8,128)(2,1)} %after.15.refs_4_), channel_id=1, source_target_pairs={{0,16},{8,24},{16,0},{24,8},{1,17},{9,25},{17,1},{25,9},{2,18},{10... | collective-permute-start | bytes 5111816 | tf_op jit(solution)/shard_map/ppermute | solution.py:672
  52.2 50.5 %collective-permute-start.8 = (bf16[4,384,512]{2,1,0:T(8,128)(2,1)}, bf16[4,384,512]{2,1,0:T(8,128)(2,1)}, u32[]{:S(2)}, u32[]{:S(2)}) collective-permute-start(bf16[4,384,512]{2,1,0:T(8,128)(2,1)} %after.12), channel_id=1, source_target_pairs={{0,1},{1,0},{2,3},{3,2},{4,5},{5,4},{6,7},{7,6},{8,9},{9,8},{10,11... | collective-permute-start | bytes 4718600 | tf_op jit(solution)/shard_map/ppermute | solution.py:585
  52.6 7.9 %copy-start.8 = (s32[8,8]{1,0:T(8,128)S(1)}, s32[8,8]{1,0:T(8,128)}, u32[]{:S(2)}) copy-start(s32[8,8]{1,0:T(8,128)} %copy-done.7) | copy-start | bytes 772
  52.6 8.5 %copy-start.12 = (s32[8,8]{1,0:T(8,128)S(1)}, s32[8,8]{1,0:T(8,128)}, u32[]{:S(2)}) copy-start(s32[8,8]{1,0:T(8,128)} %copy-done.11) | copy-start | bytes 772
  52.6 9.1 %copy-start.17 = (s32[8,8]{1,0:T(8,128)S(1)}, s32[8,8]{1,0:T(8,128)}, u32[]{:S(2)}) copy-start(s32[8,8]{1,0:T(8,128)} %get-tuple-element.124) | copy-start | bytes 772
  52.6 50.1 %collective-permute-start.9 = (bf16[4,384,512]{2,1,0:T(8,128)(2,1)}, bf16[4,384,512]{2,1,0:T(8,128)(2,1)}, u32[]{:S(2)}, u32[]{:S(2)}) collective-permute-start(bf16[4,384,512]{2,1,0:T(8,128)(2,1)} %after.13.refs_1_), channel_id=1, source_target_pairs={{2,4},{3,5},{4,6},{5,7},{10,12},{11,13},{12,14},{13,15},{18,20},{1... | collective-permute-start | bytes 4718600 | tf_op jit(solution)/shard_map/ppermute | solution.py:591
  54.7 12.1 %copy-start.5 = (s32[24,128]{1,0:T(8,128)S(1)}, s32[24,128]{1,0:T(8,128)}, u32[]{:S(2)}) copy-start(s32[24,128]{1,0:T(8,128)} %copy-done.4) | copy-start | bytes 36868
  54.7 12.1 %copy-start.6 = (s32[8,384]{1,0:T(8,128)S(1)}, s32[8,384]{1,0:T(8,128)}, u32[]{:S(2)}) copy-start(s32[8,384]{1,0:T(8,128)} %get-tuple-element.94) | copy-start | bytes 36868
  54.7 48.0 %collective-permute-start.10 = (bf16[4,384,512]{2,1,0:T(8,128)(2,1)}, bf16[4,384,512]{2,1,0:T(8,128)(2,1)}, u32[]{:S(2)}, u32[]{:S(2)}) collective-permute-start(bf16[4,384,512]{2,1,0:T(8,128)(2,1)} %after.14.refs_4_), channel_id=1, source_target_pairs={{2,0},{3,1},{4,2},{5,3},{10,8},{11,9},{12,10},{13,11},{18,16},{19,... | collective-permute-start | bytes 4718600 | tf_op jit(solution)/shard_map/ppermute | solution.py:592
  62.4 1.2 copy-start.2
  64.2 38.6 %collective-permute-start.12 = (bf16[40,4,16,128]{3,2,1,0:T(8,128)(2,1)}, bf16[40,4,16,128]{3,2,1,0:T(8,128)(2,1)}, u32[]{:S(2)}, u32[]{:S(2)}) collective-permute-start(bf16[40,4,16,128]{3,2,1,0:T(8,128)(2,1)} %after.16.refs_2_), channel_id=1, source_target_pairs={{0,8},{8,0},{16,24},{24,16},{1,9},{9,1},{17,25},{25,17},{2,10},{10... | collective-permute-start | bytes 1966088 | tf_op jit(solution)/shard_map/ppermute | solution.py:684
  103.4 8.2 %collective-permute-start.16 = (bf16[112,4,16,128]{3,2,1,0:T(8,128)(2,1)}, bf16[112,4,16,128]{3,2,1,0:T(8,128)(2,1)S(1)}, u32[]{:S(2)}, u32[]{:S(2)}) collective-permute-start(bf16[112,4,16,128]{3,2,1,0:T(8,128)(2,1)} %after.17.refs_8_), channel_id=1, source_target_pairs={{0,8},{8,0},{16,24},{24,16},{1,9},{9,1},{17,25},{25,17},{2,10},{10... | collective-permute-start | bytes 5505032 | tf_op jit(solution)/shard_map/ppermute | solution.py:672
  106.1 35.2 %collective-permute-start.20 = (bf16[4,384,512]{2,1,0:T(8,128)(2,1)}, bf16[4,384,512]{2,1,0:T(8,128)(2,1)}, u32[]{:S(2)}, u32[]{:S(2)}) collective-permute-start(bf16[4,384,512]{2,1,0:T(8,128)(2,1)} %after.19.refs_2_), channel_id=1, source_target_pairs={{4,6},{5,7},{12,14},{13,15},{20,22},{21,23},{28,30},{29,31}} | collective-permute-start | bytes 4718600 | tf_op jit(solution)/shard_map/ppermute | solution.py:591
  108.6 41.4 %collective-permute-start.18 = (bf16[112,4,16,128]{3,2,1,0:T(8,128)(2,1)}, bf16[112,4,16,128]{3,2,1,0:T(8,128)(2,1)}, u32[]{:S(2)}, u32[]{:S(2)}) collective-permute-start(bf16[112,4,16,128]{3,2,1,0:T(8,128)(2,1)} %after.17.refs_8_), channel_id=1, source_target_pairs={{0,16},{8,24},{16,0},{24,8},{1,17},{9,25},{17,1},{25,9},{2,18},{10... | collective-permute-start | bytes 5505032 | tf_op jit(solution)/shard_map/ppermute | solution.py:672
  109.8 42.5 %collective-permute-start.21 = (bf16[4,384,512]{2,1,0:T(8,128)(2,1)}, bf16[4,384,512]{2,1,0:T(8,128)(2,1)}, u32[]{:S(2)}, u32[]{:S(2)}) collective-permute-start(bf16[4,384,512]{2,1,0:T(8,128)(2,1)} %after.20.refs_5_), channel_id=1, source_target_pairs={{2,0},{3,1},{10,8},{11,9},{18,16},{19,17},{26,24},{27,25}} | collective-permute-start | bytes 4718600 | tf_op jit(solution)/shard_map/ppermute | solution.py:592
  111.6 1.2 copy-start.1
  113.4 42.2 %collective-permute-start.17 = (bf16[104,4,16,128]{3,2,1,0:T(8,128)(2,1)}, bf16[104,4,16,128]{3,2,1,0:T(8,128)(2,1)}, u32[]{:S(2)}, u32[]{:S(2)}) collective-permute-start(bf16[104,4,16,128]{3,2,1,0:T(8,128)(2,1)} %after.18.refs_6_), channel_id=1, source_target_pairs={{0,8},{8,0},{16,24},{24,16},{1,9},{9,1},{17,25},{25,17},{2,10},{10... | collective-permute-start | bytes 5111816 | tf_op jit(solution)/shard_map/ppermute | solution.py:684
  114.2 41.4 %collective-permute-start.22 = (bf16[4,384,512]{2,1,0:T(8,128)(2,1)}, bf16[4,384,512]{2,1,0:T(8,128)(2,1)}, u32[]{:S(2)}, u32[]{:S(2)}) collective-permute-start(bf16[4,384,512]{2,1,0:T(8,128)(2,1)} %after.21), channel_id=1, source_target_pairs={{0,1},{1,0},{2,3},{3,2},{4,5},{5,4},{6,7},{7,6},{8,9},{9,8},{10,11... | collective-permute-start | bytes 4718600 | tf_op jit(solution)/shard_map/ppermute | solution.py:585
  141.3 83.4 %collective-permute-start.15 = (bf16[192,4,16,128]{3,2,1,0:T(8,128)(2,1)}, bf16[192,4,16,128]{3,2,1,0:T(8,128)(2,1)S(1)}, u32[]{:S(2)}, u32[]{:S(2)}) collective-permute-start(bf16[192,4,16,128]{3,2,1,0:T(8,128)(2,1)} %compact.9.refs_6_.refs_0_), channel_id=1, source_target_pairs={{0,16},{8,24},{16,0},{24,8},{1,17},{9,25},{17,1},{25,9},{2,18},{10... | collective-permute-start | bytes 9437192 | tf_op jit(solution)/shard_map/ppermute | solution.py:672
  150.0 50.3 %collective-permute-start.19 = (bf16[112,4,16,128]{3,2,1,0:T(8,128)(2,1)}, bf16[112,4,16,128]{3,2,1,0:T(8,128)(2,1)}, u32[]{:S(2)}, u32[]{:S(2)}) collective-permute-start(bf16[112,4,16,128]{3,2,1,0:T(8,128)(2,1)} %collective-permute-done.18.refs_4_.refs_10_), channel_id=1, source_target_pairs={{0,8},{8,0},{16,24},{24,16},{1,9},{9,1},{17,25},{25,17},{2,10},{10... | collective-permute-start | bytes 5505032 | tf_op jit(solution)/shard_map/ppermute | solution.py:700
  156.2 1.9 copy-start.19
  156.2 37.0 %collective-permute-start.23 = (bf16[4,384,512]{2,1,0:T(8,128)(2,1)}, bf16[4,384,512]{2,1,0:T(8,128)(2,1)}, u32[]{:S(2)}, u32[]{:S(2)}) collective-permute-start(bf16[4,384,512]{2,1,0:T(8,128)(2,1)} %after.22), channel_id=1, source_target_pairs={{0,1},{1,0},{2,3},{3,2},{4,5},{5,4},{6,7},{7,6},{8,9},{9,8},{10,11... | collective-permute-start | bytes 4718600 | tf_op jit(solution)/shard_map/ppermute | solution.py:585
  161.4 68.8 %collective-permute-start.14 = (bf16[192,4,16,128]{3,2,1,0:T(8,128)(2,1)}, bf16[192,4,16,128]{3,2,1,0:T(8,128)(2,1)}, u32[]{:S(2)}, u32[]{:S(2)}) collective-permute-start(bf16[192,4,16,128]{3,2,1,0:T(8,128)(2,1)} %compact.9.refs_6_.refs_0_), channel_id=1, source_target_pairs={{0,8},{8,0},{16,24},{24,16},{1,9},{9,1},{17,25},{25,17},{2,10},{10... | collective-permute-start | bytes 9437192 | tf_op jit(solution)/shard_map/ppermute | solution.py:672
  224.7 2.2 copy-start.10
  224.7 2.8 %copy-start.14 = (s32[8]{0:T(128)S(1)}, s32[8]{0:T(128)}, u32[]{:S(2)}) copy-start(s32[8]{0:T(128)} %copy-done.13) | copy-start | bytes 100
  224.7 2.8 %copy-start.21 = (s32[8]{0:T(128)S(1)}, s32[8]{0:T(128)}, u32[]{:S(2)}) copy-start(s32[8]{0:T(128)} %copy-done.20) | copy-start | bytes 100
  224.7 4.8 %copy-start.16 = (s32[528]{0:T(1024)S(1)}, s32[528]{0:T(1024)}, u32[]{:S(2)}) copy-start(s32[528]{0:T(1024)} %get-tuple-element.127) | copy-start | bytes 6340
  224.8 1.6 copy-start.3
  226.4 6.2 %collective-permute-start.24 = (bf16[192,4,16,128]{3,2,1,0:T(8,128)(2,1)}, bf16[192,4,16,128]{3,2,1,0:T(8,128)(2,1)}, u32[]{:S(2)}, u32[]{:S(2)}) collective-permute-start(bf16[192,4,16,128]{3,2,1,0:T(8,128)(2,1)} %after.23.refs_2_), channel_id=1, source_target_pairs={{0,8},{8,0},{16,24},{24,16},{1,9},{9,1},{17,25},{25,17},{2,10},{10... | collective-permute-start | bytes 9437192 | tf_op jit(solution)/shard_map/ppermute | solution.py:716
